TPU v7x, 256 devices: a whole 4x4x8 slice. The times are simulated.
256 devices in a mesh: ctx: 16 (over x, y), exp: 16 (over z, core).
Axes of the slice: x: 4, y: 4, z: 8, core: 2. Of those that a mesh axis runs over, the one named last changes fastest.
Arguments:
- u_in: bfloat16 [4096, 8192], P('ctx', 'exp'), may hold values from -6 to 6
- z_gate: bfloat16 [4096, 8192], P('ctx', 'exp'), may hold values from -6 to 6
- delta: float32 [4096, 8192], P('ctx', 'exp'), may hold values from 0.125 to 8, as said below
- b_in: float32 [4096, 16], P('ctx'), may hold values from -1.5 to 1.5
- c_in: float32 [4096, 16], P('ctx'), may hold values from -1.5 to 1.5
- rate: float32 [16, 8192], P(None, 'exp'), may hold values from 0.00024414062 to 0.05
- skip: float32 [8192], P('exp'), may hold values from 0.5 to 1.5
- w_out: bfloat16 [8192, 2048], P('exp'), may hold values from -0.015625 to 0.015625
- resid: bfloat16 [4096, 2048], P(('ctx', 'exp')), may hold values from -6 to 6
- gain: float32 [2048], replicated, may hold values from 0.5 to 1.5
- expert_ids: int32 [4096, 2], P(('ctx', 'exp')), may hold values from 0 to 15, all different within a row; in each aligned block of 16 rows (0 to 15, 16 to 31, ...) at most 4 rows name the same one
- route_weights: float32 [4096, 2], P(('ctx', 'exp')), may hold values from 0.2 to 1
- w_gate: bfloat16 [16, 2048, 8192], P('exp', None, 'ctx'), may hold values from -0.125 to 0.125
- w_up: bfloat16 [16, 2048, 8192], P('exp', None, 'ctx'), may hold values from -0.125 to 0.125
- w_down: bfloat16 [16, 8192, 2048], P('exp', 'ctx'), may hold values from -0.0625 to 0.0625
- d_out: bfloat16 [4096, 2048], P(('ctx', 'exp')), may hold values from -6 to 6
Outputs:
- final: bfloat16 [4096, 2048], P(('ctx', 'exp'))
- grad_resid: bfloat16 [4096, 2048], P(('ctx', 'exp'))
- grad_u: bfloat16 [4096, 8192], P('ctx', 'exp')
Inputs may be any that keep to these rules, and one draw needn't show every extreme that they name: `expert_ids`: in each aligned block of 16 rows (the rows of one device) no expert is named by more than 4 rows, a bound that some block reaches; the two ids of a row differ. `delta`: positive step sizes.
All inputs are finite; a program needn't handle non-finite values.
Results may differ from a plain program's by a relative error of at most 0.025.
Values may be sent and summed in bfloat16 or wider, within the bound.
A program may use at most 128 MiB of HBM per device.

v0:
```python
import jax
import jax.numpy as jnp
from jax import lax
from jax.sharding import PartitionSpec as P


def prefix(value, axis, join, neutral, backward):
    count = lax.axis_size(axis)
    place = lax.axis_index(axis)
    ahead = count - 1 - place if backward else place
    gathered = jax.tree.map(
        lambda a, kind: lax.all_gather(a.astype(kind), axis), value, (jnp.bfloat16, jnp.bfloat16)
    )
    state = jax.tree.map(lambda a, e: jnp.zeros_like(a) + jnp.asarray(e, a.dtype), value, neutral)

    def one(turn, state):
        source = count - 1 - turn if backward else turn
        return join(
            state,
            jax.tree.map(
                lambda a, own: lax.dynamic_index_in_dim(a, source, 0, False).astype(own.dtype),
                gathered,
                value,
            ),
        )

    return lax.fori_loop(0, ahead, one, state)


def affine_join(earlier, later):
    return (earlier[0] * later[0], later[0] * earlier[1] + later[1])


def contract_last(left, right):
    return lax.dot_general(
        left, right, (((1,), (1,)), ((), ())), preferred_element_type=jnp.float32
    )


def forward_blocks(cumul, start_cum, drive, b_in, c_in, rate, state_in, sub):
    seg_rows, channels = drive.shape
    count = seg_rows // sub
    lower = jnp.arange(sub)[:, None] >= jnp.arange(sub)[None, :]
    lower_f = lower.astype(jnp.float32)

    def forward_advance(carried, inputs):
        cum, base, drv, b_rows, c_rows = inputs
        spread = jnp.where(lower[:, :, None], cum[:, None, :] - cum[None, :, :], 0.0)
        weight = jnp.exp(-rate[None, None] * spread[:, :, None, :]) * lower_f[:, :, None, None]
        source = b_rows[:, :, None] * drv[:, None, :]
        inner = jnp.sum(weight * source[None], axis=1)
        enter = jnp.exp(-rate[None] * (cum - base[None])[:, None, :])
        states = inner + enter * carried[None]
        output = jnp.sum(c_rows[:, :, None] * states, axis=1)
        last = cum[-1]
        fade = jnp.exp(-rate[None] * (last[None] - cum)[:, None, :])
        updated = jnp.exp(-rate * (last - base)[None]) * carried + jnp.sum(fade * source, axis=0)
        return (updated, output)

    inputs = (
        cumul.reshape(count, sub, channels),
        start_cum,
        drive.reshape(count, sub, channels),
        b_in.reshape(count, sub, -1),
        c_in.reshape(count, sub, -1),
    )
    _, outputs = lax.scan(forward_advance, state_in, inputs)
    return outputs.reshape(seg_rows, channels)


def backward_blocks(cumul, start_cum, out_grad, delta, b_in, c_in, rate, grad_in, sub):
    seg_rows, channels = out_grad.shape
    count = seg_rows // sub
    upper = jnp.arange(sub)[:, None] <= jnp.arange(sub)[None, :]
    upper_f = upper.astype(jnp.float32)

    def backward_advance(carried, inputs):
        cum, base, grad_rows, step_rows, b_rows, c_rows = inputs
        spread = jnp.where(upper[:, :, None], cum[None, :, :] - cum[:, None, :], 0.0)
        weight = jnp.exp(-rate[None, None] * spread[:, :, None, :]) * upper_f[:, :, None, None]
        source = c_rows[:, :, None] * grad_rows[:, None, :]
        last = cum[-1]
        adjoint = jnp.sum(weight * source[None], axis=1)
        adjoint = adjoint + jnp.exp(-rate[None] * (last[None] - cum)[:, None, :]) * carried[None]
        output = jnp.sum(b_rows[:, :, None] * adjoint, axis=1) * step_rows
        fade = jnp.exp(-rate[None] * (cum - base[None])[:, None, :])
        updated = jnp.sum(fade * source, axis=0) + jnp.exp(-rate * (last - base)[None]) * carried
        return (updated, output)

    inputs = (
        cumul.reshape(count, sub, channels),
        start_cum,
        out_grad.reshape(count, sub, channels),
        delta.reshape(count, sub, channels),
        b_in.reshape(count, sub, -1),
        c_in.reshape(count, sub, -1),
    )
    _, outputs = lax.scan(backward_advance, grad_in, inputs, reverse=True)
    return outputs.reshape(seg_rows, channels)


def local(
    u_in,
    z_gate,
    delta,
    b_in,
    c_in,
    rate,
    skip,
    w_out,
    resid,
    gain,
    expert_ids,
    route_weights,
    w_gate,
    w_up,
    w_down,
    d_out,
):
    seg_rows, channels = u_in.shape
    my_rows, width = resid.shape
    experts_count = lax.axis_size("exp")
    capacity = 4 * my_rows // experts_count
    sub = min(16, seg_rows)
    sub_count = seg_rows // sub
    u_float = u_in.astype(jnp.float32)
    z_act = jax.nn.silu(z_gate.astype(jnp.float32))
    steps_index = jnp.arange(seg_rows)
    lower = (steps_index[:, None] >= steps_index[None, :]).astype(jnp.float32)
    cumul = jnp.dot(lower, delta, precision=lax.Precision.HIGHEST)
    exclusive = cumul - delta
    start_cum = exclusive.reshape(sub_count, sub, channels)[:, 0]
    last_sum = cumul[-1]
    drive = delta * u_float
    decay_all = jnp.exp(-rate * last_sum[None, :])
    tail = jnp.exp(-rate[None, :, :] * (last_sum[None, :] - cumul)[:, None, :])
    state_end = jnp.sum(tail * b_in[:, :, None] * drive[:, None, :], axis=0)
    identity = (jnp.ones_like(decay_all), jnp.zeros_like(state_end))
    _, state_in = prefix((decay_all, state_end), "ctx", affine_join, identity, False)
    scanned = forward_blocks(cumul, start_cum, drive, b_in, c_in, rate, state_in, sub)
    scanned = scanned + skip[None, :] * u_float
    gated = (scanned * z_act).astype(jnp.bfloat16)
    mixed = lax.psum_scatter(
        jnp.dot(gated, w_out, preferred_element_type=jnp.float32).astype(jnp.bfloat16),
        "exp",
        scatter_dimension=0,
        tiled=True,
    ).astype(jnp.float32)
    stream = resid.astype(jnp.float32) + mixed
    inverse = lax.rsqrt(jnp.mean(stream * stream, axis=-1, keepdims=True) + 1e-05)
    normed = (stream * inverse * gain[None, :]).astype(jnp.bfloat16)
    owners = expert_ids.reshape(-1)
    assign_count = owners.shape[0]
    onehot = (owners[:, None] == jnp.arange(experts_count, dtype=jnp.int32)[None, :]).astype(
        jnp.float32
    )
    assign_index = jnp.arange(assign_count)
    strict = (assign_index[:, None] > assign_index[None, :]).astype(jnp.float32)
    before = jnp.dot(strict, onehot, precision=lax.Precision.HIGHEST)
    slots = jnp.sum(before * onehot, axis=1).astype(jnp.int32)
    target = owners * capacity + slots
    placing = (
        jnp.arange(experts_count * capacity, dtype=jnp.int32)[:, None] == target[None, :]
    ).astype(jnp.bfloat16)
    paired = jnp.repeat(normed, 2, axis=0)
    outgoing = (
        jnp.dot(placing, paired, preferred_element_type=jnp.float32)
        .astype(jnp.bfloat16)
        .reshape(experts_count, capacity, width)
    )
    cotangent = (
        route_weights.reshape(-1)[:, None] * jnp.repeat(d_out.astype(jnp.float32), 2, axis=0)
    ).astype(jnp.bfloat16)
    grad_outgoing = (
        jnp.dot(placing, cotangent, preferred_element_type=jnp.float32)
        .astype(jnp.bfloat16)
        .reshape(experts_count, capacity, width)
    )
    arrived = lax.all_to_all(outgoing, "exp", split_axis=0, concat_axis=0, tiled=True)
    every_rows = lax.all_gather(arrived, "ctx", axis=0, tiled=True)
    flat_rows = every_rows.reshape(-1, width)
    gate_pre = jnp.dot(flat_rows, w_gate[0], preferred_element_type=jnp.float32)
    up_pre = jnp.dot(flat_rows, w_up[0], preferred_element_type=jnp.float32)
    sigma = jax.nn.sigmoid(gate_pre)
    active = gate_pre * sigma
    hidden_act = (active * up_pre).astype(jnp.bfloat16)
    partial_out = jnp.dot(hidden_act, w_down[0], preferred_element_type=jnp.float32).reshape(
        every_rows.shape
    )
    summed = lax.psum_scatter(
        partial_out.astype(jnp.bfloat16), "ctx", scatter_dimension=0, tiled=True
    )
    returned = lax.all_to_all(summed, "exp", split_axis=0, concat_axis=0, tiled=True)
    expert_out = lax.dot_general(
        placing,
        returned.reshape(-1, width),
        (((0,), (0,)), ((), ())),
        preferred_element_type=jnp.float32,
    )
    expert_out = expert_out.reshape(my_rows, 2, width)
    final = (
        stream + route_weights[:, 0:1] * expert_out[:, 0] + route_weights[:, 1:2] * expert_out[:, 1]
    ).astype(jnp.bfloat16)
    grad_arrived = lax.all_to_all(grad_outgoing, "exp", split_axis=0, concat_axis=0, tiled=True)
    every_grad = lax.all_gather(grad_arrived, "ctx", axis=0, tiled=True)
    flat_grad = every_grad.reshape(-1, width)
    hidden_grad = contract_last(flat_grad, w_down[0])
    gate_grad = (hidden_grad * up_pre * sigma * (1.0 + gate_pre * (1.0 - sigma))).astype(
        jnp.bfloat16
    )
    up_grad = (hidden_grad * active).astype(jnp.bfloat16)
    row_terms = contract_last(gate_grad, w_gate[0]) + contract_last(up_grad, w_up[0])
    row_sums = lax.psum_scatter(
        row_terms.reshape(every_rows.shape).astype(jnp.bfloat16),
        "ctx",
        scatter_dimension=0,
        tiled=True,
    )
    grad_back = lax.all_to_all(row_sums, "exp", split_axis=0, concat_axis=0, tiled=True)
    normed_grad = lax.dot_general(
        placing,
        grad_back.reshape(-1, width),
        (((0,), (0,)), ((), ())),
        preferred_element_type=jnp.float32,
    )
    normed_grad = normed_grad.reshape(my_rows, 2, width)
    normed_grad = normed_grad[:, 0] + normed_grad[:, 1]
    scaled = normed_grad * gain[None, :]
    project_mean = jnp.mean(scaled * stream, axis=-1, keepdims=True)
    stream_grad = inverse * (scaled - stream * inverse * inverse * project_mean)
    grad_resid = (d_out.astype(jnp.float32) + stream_grad).astype(jnp.bfloat16)
    segment_grad = lax.all_gather(grad_resid, "exp", axis=0, tiled=True)
    out_grad = contract_last(segment_grad, w_out) * z_act
    head = jnp.exp(-rate[None, :, :] * cumul[:, None, :])
    back_end = jnp.sum(head * c_in[:, :, None] * out_grad[:, None, :], axis=0)
    _, grad_in = prefix((decay_all, back_end), "ctx", affine_join, identity, True)
    back_terms = backward_blocks(cumul, start_cum, out_grad, delta, b_in, c_in, rate, grad_in, sub)
    grad_u = (back_terms + skip[None, :] * out_grad).astype(jnp.bfloat16)
    return (final, grad_resid, grad_u)


def solution(mesh):
    return jax.shard_map(
        local,
        mesh=mesh,
        in_specs=(
            P("ctx", "exp"),
            P("ctx", "exp"),
            P("ctx", "exp"),
            P("ctx", None),
            P("ctx", None),
            P(None, "exp"),
            P("exp"),
            P("exp", None),
            P(("ctx", "exp"), None),
            P(),
            P(("ctx", "exp"), None),
            P(("ctx", "exp"), None),
            P("exp", None, "ctx"),
            P("exp", None, "ctx"),
            P("exp", "ctx", None),
            P(("ctx", "exp"), None),
        ),
        out_specs=(P(("ctx", "exp"), None), P(("ctx", "exp"), None), P("ctx", "exp")),
        check_vma=False,
    )
```

profile of v0, /device:TPU:1, one launch (start us, length us, event | category | flops | bytes accessed | tf_op | source)
XLA Modules:
  0.0 733.4 jit_solution(11654428361903023195)
XLA Ops:
  14.1 19.7 %all-gather = bf16[256,512]{1,0:T(8,128)(2,1)S(1)} all-gather(bf16[16,512]{1,0:T(8,128)(2,1)S(1)} %get-tuple-element.676), channel_id=2, replica_groups=mesh['ctx'=16,'exp'=16] {'ctx'}, dimensions={0}, use_global_device_ids=true | all-gather | bytes 278528 | tf_op jit(solution)/shard_map/all_gather | solution.py:12
  36.8 19.2 %all-gather.1 = bf16[256,512]{1,0:T(8,128)(2,1)} all-gather(bf16[16,512]{1,0:T(8,128)(2,1)S(1)} %multiply_reduce_fusion.7), channel_id=3, replica_groups=mesh['ctx'=16,'exp'=16] {'ctx'}, dimensions={0}, use_global_device_ids=true | all-gather | bytes 278528 | tf_op jit(solution)/shard_map/all_gather | solution.py:12
  56.9 90.2 %while.60 = (s32[]{:T(128)}, f32[16,512]{1,0:T(8,128)S(1)}, f32[16,16,512]{2,1,0:T(8,128)}, f32[16,16,512]{2,1,0:T(8,128)S(1)}, f32[16,512]{1,0:T(8,128)S(1)}, /...) while((s32[]{:T(128)}, f32[16,512]{1,0:T(8,128)S(1)}, ...), condition=%wide.region_7.8_spmd.clone, body=%wide.region_3.7_spmd.clone.sunk | while | flops 9856259 | bytes 3925681 | solution.py:67
  58.7 2.9 multiply_reduce_fusion.14
  75.6 2.9 multiply_reduce_fusion.14
  81.3 2.9 multiply_reduce_fusion.14
  92.5 2.9 multiply_reduce_fusion.14
  103.8 2.9 multiply_reduce_fusion.14
  148.4 3.3 convolution_convert_fusion.1
  156.2 32.0 %all_to_all.20 = bf16[16,4,2048]{2,1,0:T(4,128)(2,1)} all-to-all(bf16[16,4,2048]{2,1,0:T(4,128)(2,1)} %reshape.345), channel_id=1, replica_groups=mesh['ctx'=16,'exp'=16] {'exp'}, dimensions={0} | all-to-all | bytes 524288 | tf_op jit(solution)/shard_map/all_to_all | solution.py:204
  188.3 40.3 %reduce-scatter.3.cloned.1.call-done = bf16[16,2048]{1,0:T(8,128)(2,1)} async-done(((bf16[256,2048]{1,0:T(8,128)(2,1)}), bf16[16,2048]{1,0:T(8,128)(2,1)}) %reduce-scatter.3.cloned.1.call-update) | async-done | bytes 65552 | tf_op jit(solution)/shard_map/reduce_scatter | solution.py:143
  233.3 19.5 %all_to_all.21 = bf16[16,4,2048]{2,1,0:T(4,128)(2,1)} all-to-all(bf16[16,4,2048]{2,1,0:T(4,128)(2,1)} %reshape.341), channel_id=1, replica_groups=mesh['ctx'=16,'exp'=16] {'exp'}, dimensions={0} | all-to-all | bytes 524288 | tf_op jit(solution)/shard_map/all_to_all | solution.py:179
  253.0 6.9 reshape.346
  259.9 6.6 fusion.12
  266.5 42.4 %all-gather.7.cloned.1.call-done = bf16[256,4,2048]{2,1,0:T(4,128)(2,1)} async-done(((bf16[16,4,2048]{2,1,0:T(4,128)(2,1)}), bf16[256,4,2048]{2,1,0:T(4,128)(2,1)}) %all-gather.7.cloned.1.call-update) | async-done | bytes 4194320 | tf_op jit(solution)/shard_map/all_gather | solution.py:180
  308.9 6.9 reshape.342
  315.9 5.3 fusion.19
  321.2 3.7 multiply_convert_fusion.2
  324.9 2.9 fusion.17
  327.8 4.5 add_convert_fusion
  332.3 7.2 convert_element_type.164
  341.8 6.2 convolution_convert_fusion
  350.0 102.4 %all-reduce.3.cloned.1.call-done = bf16[256,4,2048]{2,1,0:T(4,128)(2,1)} async-done(((bf16[256,4,2048]{2,1,0:T(4,128)(2,1)}), bf16[256,4,2048]{2,1,0:T(4,128)(2,1)}) %all-reduce.3.cloned.1.call-update) | async-done | bytes 4194320
  454.2 8.0 %all-to-all-start.3 = ((bf16[16,4,2048]{2,1,0:T(4,128)(2,1)}), bf16[16,4,2048]{2,1,0:T(4,128)(2,1)S(1)}, u32[]{:S(2)}, u32[]{:S(2)}) async-start(bf16[16,4,2048]{2,1,0:T(4,128)(2,1)} %constant_dynamic-slice_fusion.4), calls=%async_computation.5 | async-start | bytes 524288 | tf_op jit(solution)/shard_map/all_to_all | solution.py:219
  462.2 11.6 %all-to-all-done.3 = bf16[16,4,2048]{2,1,0:T(4,128)(2,1)S(1)} async-done(((bf16[16,4,2048]{2,1,0:T(4,128)(2,1)}), bf16[16,4,2048]{2,1,0:T(4,128)(2,1)S(1)}, u32[]{:S(2)}, u32[]{:S(2)}) %all-to-all-start.3) | async-done | bytes 262176 | tf_op jit(solution)/shard_map/all_to_all | solution.py:219
  474.6 62.9 %reduce-scatter.5.cloned.1.call-done = bf16[16,4,2048]{2,0,1:T(8,128)(2,1)} async-done(((bf16[256,4,2048]{2,0,1:T(8,128)(2,1)}), bf16[16,4,2048]{2,0,1:T(8,128)(2,1)}) %reduce-scatter.5.cloned.1.call-update) | async-done | bytes 262160 | tf_op jit(solution)/shard_map/reduce_scatter | solution.py:190
  539.4 9.4 %all-to-all-start.1 = ((bf16[16,4,2048]{2,1,0:T(4,128)(2,1)}), bf16[16,4,2048]{2,1,0:T(4,128)(2,1)}, u32[]{:S(2)}, u32[]{:S(2)}) async-start(bf16[16,4,2048]{2,1,0:T(4,128)(2,1)} %copy.55), calls=%async_computation.3 | async-start | bytes 524288 | tf_op jit(solution)/shard_map/all_to_all | solution.py:193
  551.0 9.6 %all-to-all-done.1 = bf16[16,4,2048]{2,1,0:T(4,128)(2,1)} async-done(((bf16[16,4,2048]{2,1,0:T(4,128)(2,1)}), bf16[16,4,2048]{2,1,0:T(4,128)(2,1)}, u32[]{:S(2)}, u32[]{:S(2)}) %all-to-all-start.1) | async-done | bytes 262176 | tf_op jit(solution)/shard_map/all_to_all | solution.py:193
  565.1 33.6 %all-gather.11.cloned.1.call-done = bf16[256,2048]{1,0:T(8,128)(2,1)} async-done(((bf16[16,2048]{1,0:T(8,128)(2,1)}), bf16[256,2048]{1,0:T(8,128)(2,1)}) %all-gather.11.cloned.1.call-update) | async-done | bytes 1048592 | tf_op jit(solution)/shard_map/all_gather | solution.py:232
  603.2 18.5 %all-gather.2 = bf16[256,512]{1,0:T(8,128)(2,1)S(1)} all-gather(bf16[16,512]{1,0:T(8,128)(2,1)S(1)} %multiply_reduce_fusion.6), channel_id=4, replica_groups=mesh['ctx'=16,'exp'=16] {'ctx'}, dimensions={0}, use_global_device_ids=true | all-gather | bytes 278528 | tf_op jit(solution)/shard_map/all_gather | solution.py:12
  621.8 10.9 %while.59 = (s32[]{:T(128)}, f32[16,512]{1,0:T(8,128)S(1)}, s32[]{:T(128)}, bf16[16,16,512]{2,1,0:T(8,128)(2,1)}, bf16[16,16,512]{2,1,0:T(8,128)(2,1)S(1)}, /*index=5*/s32[]{:T(128)}, s32[]{:T(128)}, s32[]{:T(128)}, s32[]{:T(128)}) while((s32[]{:T(128)}, f32[16,512]{1,0:T(8,128)S(1)}, s32[]{:T(128)}, bf16[16,16,512]{2,1,0:T(8,128)(2,1)}, ...), condition=%wide.region_16.17_spmd, body=%wide.region_15.16_spmd.sunk | while | flops 32774 | bytes 98455 | solution.py:27
  633.6 90.2 %while.61 = (s32[]{:T(128)}, f32[16,512]{1,0:T(8,128)S(1)}, f32[16,16,512]{2,1,0:T(8,128)}, f32[1,16,512]{2,1,0:T(8,128)S(1)}, f32[16,16,512]{2,1,0:T(8,128)S(1)...) while((s32[]{:T(128)}, f32[16,512]{1,0:T(8,128)S(1)}, ...), condition=%wide.region_21.22_spmd.clone, body=%wide.region_17.21_spmd.clone.sunk | while | flops 9864452 | bytes 3958469 | solution.py:98
  (520 shorter events, 217.9 us)
Async XLA Ops:
  8.0 313.2 %copy-start = (bf16[1,2048,512]{2,1,0:T(8,128)(2,1)S(1)}, bf16[1,2048,512]{2,1,0:T(8,128)(2,1)}, u32[]{:S(2)}) copy-start(bf16[1,2048,512]{2,1,0:T(8,128)(2,1)} %param.37) | copy-start | bytes 6291460
  8.0 25.8 %copy-start.2 = (f32[256,512]{1,0:T(8,128)S(1)}, f32[256,512]{1,0:T(8,128)}, u32[]{:S(2)}) copy-start(f32[256,512]{1,0:T(8,128)} %param.26) | copy-start | bytes 1572868
  8.0 220.5 %reduce-scatter.3.cloned.1.call-start = ((), (), s32[]{:S(2)}) async-start(), calls=%async_computation.6 | async-start | bytes 1114112 | tf_op jit(solution)/shard_map/reduce_scatter | solution.py:143
  11.2 23.7 %copy-start.7 = (f32[256,16]{1,0:T(8,128)S(1)}, f32[256,16]{1,0:T(8,128)}, u32[]{:S(2)}) copy-start(f32[256,16]{1,0:T(8,128)} %copy.49) | copy-start | bytes 49156
  34.9 21.1 %copy-start.5 = (f32[256,512]{1,0:T(8,128)}, f32[256,512]{1,0:T(8,128)S(1)}, u32[]{:S(2)}) copy-start(f32[256,512]{1,0:T(8,128)S(1)} %get-tuple-element.671) | copy-start | bytes 1572868
  56.0 0.9 copy-start.6
  56.9 90.2 %copy-start.3 = (bf16[256,512]{1,0:T(8,128)(2,1)S(1)}, bf16[256,512]{1,0:T(8,128)(2,1)}, u32[]{:S(2)}) copy-start(bf16[256,512]{1,0:T(8,128)(2,1)} %param.24) | copy-start | bytes 786436
  56.9 90.2 %copy-start.10 = (f32[512]{0:T(512)S(1)}, f32[512]{0:T(512)}, u32[]{:S(2)}) copy-start(f32[512]{0:T(512)} %param.30) | copy-start | bytes 6148
  148.4 3.4 copy-start.12
  148.4 3.6 copy-start.11
  151.7 77.8 %copy-start.9 = (f32[2048]{0:T(1024)S(1)}, f32[2048]{0:T(1024)}, u32[]{:S(2)}) copy-start(f32[2048]{0:T(1024)} %param.33) | copy-start | bytes 24580
  151.7 101.3 %all-gather.9.cloned.1.call-start = ((), (), s32[]{:S(2)}) async-start(), calls=%async_computation.9 | async-start | bytes 4456448 | tf_op jit(solution)/shard_map/all_gather | solution.py:205
  188.2 120.7 %all-gather.7.cloned.1.call-start = ((), (), s32[]{:S(2)}) async-start(), calls=%async_computation.7 | async-start | bytes 4456448 | tf_op jit(solution)/shard_map/all_gather | solution.py:180
  252.8 199.6 %all-reduce.3.cloned.1.call-start = ((), (), s32[]{:S(2)}) async-start(), calls=%async_computation.11 | async-start | bytes 8388608
  315.9 5.3 copy-start.1
  321.2 3.7 copy-start.13
  321.2 3.7 copy-start.15
  339.5 198.0 %reduce-scatter.5.cloned.1.call-start = ((), (), s32[]{:S(2)}) async-start(), calls=%async_computation.8 | async-start | bytes 4456448 | tf_op jit(solution)/shard_map/reduce_scatter | solution.py:190
  348.1 0.7 copy-start.14
  454.2 19.7 %all-to-all-start.3 = ((bf16[16,4,2048]{2,1,0:T(4,128)(2,1)}), bf16[16,4,2048]{2,1,0:T(4,128)(2,1)S(1)}, u32[]{:S(2)}, u32[]{:S(2)}) async-start(bf16[16,4,2048]{2,1,0:T(4,128)(2,1)} %constant_dynamic-slice_fusion.4), calls=%async_computation.5 | async-start | bytes 524288 | tf_op jit(solution)/shard_map/all_to_all | solution.py:219
  539.4 21.2 %all-to-all-start.1 = ((bf16[16,4,2048]{2,1,0:T(4,128)(2,1)}), bf16[16,4,2048]{2,1,0:T(4,128)(2,1)}, u32[]{:S(2)}, u32[]{:S(2)}) async-start(bf16[16,4,2048]{2,1,0:T(4,128)(2,1)} %copy.55), calls=%async_computation.3 | async-start | bytes 524288 | tf_op jit(solution)/shard_map/all_to_all | solution.py:193
  548.8 49.9 %all-gather.11.cloned.1.call-start = ((), (), s32[]{:S(2)}) async-start(), calls=%async_computation.10 | async-start | bytes 1114112 | tf_op jit(solution)/shard_map/all_gather | solution.py:232
  565.1 36.3 %copy-start.8 = (f32[16,16,16]{2,1,0:T(8,128)S(1)}, f32[16,16,16]{2,1,0:T(8,128)}, u32[]{:S(2)}) copy-start(f32[16,16,16]{2,1,0:T(8,128)} %get-tuple-element.1090) | copy-start | bytes 49156
  601.4 20.4 %copy-start.4 = (f32[256,512]{1,0:T(8,128)}, f32[256,512]{1,0:T(8,128)S(1)}, u32[]{:S(2)}) copy-start(f32[256,512]{1,0:T(8,128)S(1)} %convolution_multiply_fusion) | copy-start | bytes 1572868
Sparse Core Ops, SparseCore 0:
  151.9 76.5 reduce-scatter.2
  565.3 33.4 all-gather.10
Sparse Core Ops, SparseCore 1:
  188.3 61.7 all-gather.8
  252.9 56.0 all-gather.6
  339.6 112.7 all-reduce.2
  456.5 81.0 reduce-scatter.4
where the time goes:
time: 745 us; the launch traced here: 733 us
  waiting for transfers between devices  303 us (41%)
  other arithmetic  146 us (20%)
  blocking collectives  109 us (15%)
  local copies, waits for them, and re-layouts  97.4 us (13%)
  matrix products  41.3 us (6%)
  starting transfers between devices  17.8 us (2%)
  between operations  16.7 us (2%)
    unnamed x7, waiting for transfers between devices  103 us
    reduce_scatter x1, waiting for transfers between devices, local(): lax.psum_scatter(partial_out.astype(jnp.bfloat16), 'ctx', scatter_dimensi...  62.9 us
    all_gather x3, blocking collectives, prefix(): lax.all_gather(a.astype(kind), axis)  57.4 us
    reduce_sum x16, other arithmetic, forward_advance(): inner = jnp.sum(weight * source[None], axis=1)  46 us
    reduce_sum x16, other arithmetic, backward_advance(): adjoint = jnp.sum(weight * source[None], axis=1)  46 us
    all_gather x1, waiting for transfers between devices, local(): every_rows = lax.all_gather(arrived, 'ctx', axis=0, tiled=True)  42.4 us
    reduce_scatter x1, waiting for transfers between devices, local(): lax.psum_scatter(jnp.dot(gated, w_out, preferred_element_type=jnp.float32...  40.3 us
    all_gather x1, waiting for transfers between devices, local(): segment_grad = lax.all_gather(grad_resid, 'exp', axis=0, tiled=True)  33.6 us
  transfers between devices with their start and end apart: 8, of which 7 were waited for; matrix products, arithmetic and copies ran while one was open for 5% of the time, Pallas kernels for 0%

commit v1 on v0

v1 whole, which is shorter than its diff:
```python
import functools
import math

import jax
import jax.numpy as jnp
from jax import lax
from jax.experimental import pallas as pl
from jax.experimental.pallas import tpu as pltpu
from jax.sharding import PartitionSpec as P

LANES = 128
VMEM = pl.BlockSpec(memory_space=pltpu.VMEM)
PARAMS = pltpu.CompilerParams(vmem_limit_bytes=48 * 1024 * 1024)


def contract_last(left, right):
    return lax.dot_general(
        left, right, (((1,), (1,)), ((), ())), preferred_element_type=jnp.float32
    )


def silu(v):
    return v * (1.0 / (1.0 + jnp.exp(-v)))


def tiles_of(channels):
    return [slice(i * LANES, (i + 1) * LANES) for i in range(channels // LANES)]


GROUP = 8


def scan_tokens(rows, channels, planes, step, initial, out_ref=None, backward=False):
    tiles = tiles_of(channels)
    row_index = lax.broadcasted_iota(jnp.int32, (GROUP, LANES), 0)

    def group(i, carried):
        base = rows - GROUP - i * GROUP if backward else i * GROUP
        base = pl.multiple_of(base, GROUP)
        blocks = [[plane[pl.ds(base, GROUP), tile] for plane in planes] for tile in tiles]
        made = [jnp.zeros((GROUP, LANES), jnp.float32) for _ in tiles]
        carried = list(carried)
        for j in reversed(range(GROUP)) if backward else range(GROUP):
            for k, tile in enumerate(tiles):
                line = [b[j : j + 1] for b in blocks[k]]
                carried[k], row = step(base + j, tile, line, carried[k])
                if out_ref is not None:
                    made[k] = jnp.where(row_index == j, row, made[k])
        if out_ref is not None:
            for k, tile in enumerate(tiles):
                out_ref[pl.ds(base, GROUP), tile] = made[k]
        return tuple(carried)

    return lax.fori_loop(0, rows // GROUP, group, tuple(initial))


def zero_state(rate_ref):
    states, channels = rate_ref.shape
    return [jnp.zeros((states, LANES), jnp.float32) for _ in tiles_of(channels)]


def put_state(ref, done):
    for tile, held in zip(tiles_of(ref.shape[-1]), done):
        ref[:, tile] = held


def take_state(ref):
    return [ref[:, tile] for tile in tiles_of(ref.shape[-1])]


def forward_end(delta_ref, u_ref, brep_ref, rate_ref, end_ref, sum_ref, drive_ref):
    rows, channels = delta_ref.shape
    drive_ref[...] = delta_ref[...] * u_ref[...].astype(jnp.float32)
    sum_ref[...] = jnp.sum(delta_ref[...], axis=0, keepdims=True)

    def step(t, tile, line, held):
        decay = jnp.exp2(line[0] * rate_ref[:, tile])
        return decay * held + brep_ref[t] * line[1], None

    put_state(
        end_ref, scan_tokens(rows, channels, (delta_ref, drive_ref), step, zero_state(rate_ref))
    )


def forward_out(
    delta_ref, u_ref, brep_ref, crep_ref, rate_ref, start_ref, skip_ref, z_ref, gated_ref, drive_ref, y_ref
):
    rows, channels = delta_ref.shape
    drive_ref[...] = delta_ref[...] * u_ref[...].astype(jnp.float32)

    def step(t, tile, line, held):
        decay = jnp.exp2(line[0] * rate_ref[:, tile])
        new = decay * held + brep_ref[t] * line[1]
        return new, jnp.sum(crep_ref[t] * new, axis=0, keepdims=True)

    scan_tokens(rows, channels, (delta_ref, drive_ref), step, take_state(start_ref), y_ref)
    z = z_ref[...].astype(jnp.float32)
    scanned = y_ref[...] + skip_ref[...] * u_ref[...].astype(jnp.float32)
    gated_ref[...] = (scanned * silu(z)).astype(gated_ref.dtype)


def backward_end(delta_ref, grad_ref, crep_ref, rate_ref, end_ref):
    rows, channels = delta_ref.shape

    def step(t, tile, line, held):
        decay = jnp.exp2(line[0] * rate_ref[:, tile])
        return decay * (held + crep_ref[t] * line[1]), None

    put_state(
        end_ref,
        scan_tokens(
            rows, channels, (delta_ref, grad_ref), step, zero_state(rate_ref), backward=True
        ),
    )


def backward_out(
    delta_ref, grad_ref, brep_ref, crep_ref, rate_ref, start_ref, skip_ref, out_ref, y_ref
):
    rows, channels = delta_ref.shape

    def step(t, tile, line, held):
        decay = jnp.exp2(line[0] * rate_ref[:, tile])
        new = held + crep_ref[t] * line[1]
        return decay * new, jnp.sum(brep_ref[t] * new, axis=0, keepdims=True)

    scan_tokens(
        rows, channels, (delta_ref, grad_ref), step, take_state(start_ref), y_ref, backward=True
    )
    out_ref[...] = (delta_ref[...] * y_ref[...] + skip_ref[...] * grad_ref[...]).astype(
        out_ref.dtype
    )


def local_call(body, outs, scratch, args):
    return pl.pallas_call(
        body,
        out_shape=outs,
        in_specs=[VMEM] * len(args),
        out_specs=[VMEM] * len(outs),
        scratch_shapes=scratch,
        compiler_params=PARAMS,
    )(*args)


SIDE = 4
TO_RIGHT, TO_LEFT, ON_RIGHT, ON_LEFT = 0, 1, 2, 3


class Ring:
    def __init__(self, along_x):
        c = lax.axis_index("ctx")
        x, y = c // SIDE, c % SIDE
        self.place = x if along_x else y
        up, down = (self.place + 1) % SIDE, (self.place + SIDE - 1) % SIDE
        self.after, self.before, self.across = up, down, (self.place + 2) % SIDE
        self.right = {"ctx": up * SIDE + y if along_x else x * SIDE + up}
        self.left = {"ctx": down * SIDE + y if along_x else x * SIDE + down}


def halves(ref):
    n = ref.shape[0] // 2
    return ref.at[pl.ds(0, n)], ref.at[pl.ds(n, n)]


class Gather:
    def __init__(self, ring, block, send, recv):
        self.ring, self.block, self.send, self.recv = ring, block, send, recv

    def copy(self, ref, way):
        target = self.ring.right if way in (TO_RIGHT, ON_RIGHT) else self.ring.left
        return pltpu.make_async_remote_copy(
            src_ref=ref,
            dst_ref=ref,
            send_sem=self.send.at[way],
            recv_sem=self.recv.at[way],
            device_id=target,
            device_id_type=pl.DeviceIdType.MESH,
        )

    def start(self):
        own = self.block(self.ring.place)
        self.copy(own, TO_RIGHT).start()
        self.copy(own, TO_LEFT).start()

    def before(self):
        came = self.block(self.ring.before)
        self.copy(came, TO_RIGHT).wait_recv()
        self.copy(halves(came)[0], ON_RIGHT).start()

    def after(self):
        came = self.block(self.ring.after)
        self.copy(came, TO_LEFT).wait_recv()
        self.copy(halves(came)[1], ON_LEFT).start()

    def across(self):
        first, second = halves(self.block(self.ring.across))
        self.copy(first, ON_RIGHT).wait_recv()
        self.copy(second, ON_LEFT).wait_recv()

    def finish(self):
        own = self.block(self.ring.place)
        self.copy(own, TO_RIGHT).wait_send()
        self.copy(own, TO_LEFT).wait_send()
        self.copy(halves(self.block(self.ring.before))[0], ON_RIGHT).wait_send()
        self.copy(halves(self.block(self.ring.after))[1], ON_LEFT).wait_send()


def add_into(total, term):
    total[...] = (total[...].astype(jnp.float32) + term[...].astype(jnp.float32)).astype(
        total.dtype
    )


class Reduce:
    def __init__(self, ring, part, far, near, send, recv):
        self.ring, self.part, self.far, self.near = ring, part, far, near
        self.send, self.recv = send, recv

    def copy(self, way):
        ring = self.ring
        source = {
            TO_RIGHT: lambda: halves(self.part(ring.across))[0],
            TO_LEFT: lambda: halves(self.part(ring.across))[1],
            ON_RIGHT: lambda: self.part(ring.after),
            ON_LEFT: lambda: self.part(ring.before),
        }[way]()
        target = {
            TO_RIGHT: self.far.at[0],
            TO_LEFT: self.far.at[1],
            ON_RIGHT: self.near.at[0],
            ON_LEFT: self.near.at[1],
        }[way]
        return pltpu.make_async_remote_copy(
            src_ref=source,
            dst_ref=target,
            send_sem=self.send.at[way],
            recv_sem=self.recv.at[way],
            device_id=ring.right if way in (TO_RIGHT, ON_RIGHT) else ring.left,
            device_id_type=pl.DeviceIdType.MESH,
        )

    def start(self):
        self.copy(TO_RIGHT).start()
        self.copy(TO_LEFT).start()

    def middle(self):
        self.copy(TO_RIGHT).wait_recv()
        add_into(halves(self.part(self.ring.after))[0], self.far.at[0])
        self.copy(ON_RIGHT).start()
        self.copy(TO_LEFT).wait_recv()
        add_into(halves(self.part(self.ring.before))[1], self.far.at[1])
        self.copy(ON_LEFT).start()

    def total(self):
        self.copy(ON_RIGHT).wait_recv()
        self.copy(ON_LEFT).wait_recv()
        f32 = jnp.float32
        own = self.part(self.ring.place)
        return (
            own[...].astype(f32) + self.near[0].astype(f32) + self.near[1].astype(f32)
        ).astype(own.dtype)

    def finish(self):
        for way in range(4):
            self.copy(way).wait_send()


def greet(targets):
    barrier = pltpu.get_barrier_semaphore()
    for target in targets:
        pl.semaphore_signal(
            barrier, inc=1, device_id=target, device_id_type=pl.DeviceIdType.MESH
        )
    pl.semaphore_wait(barrier, len(targets))


def experts_kernel(
    rows_ref,
    cots_ref,
    wg_ref,
    wu_ref,
    wd_ref,
    out_ref,
    grad_ref,
    held,
    parts,
    far,
    near,
    own2,
    far2,
    near2,
    send,
    recv,
):
    f32 = jnp.float32
    bf16 = jnp.bfloat16
    ring_x, ring_y = Ring(True), Ring(False)
    first = (ring_x, ring_y)
    second = (ring_y, ring_x)
    rows, width = held.shape[-2], held.shape[-1]
    greet((ring_x.right, ring_x.left, ring_y.right, ring_y.left))

    def gathers(phase):
        out = []
        for array in (1, 0):
            for half in (0, 1):
                if phase == 0:
                    block = functools.partial(
                        lambda a, h, i: held.at[a, h, second[h].place, i], array, half
                    )
                    ring = first[half]
                else:
                    block = functools.partial(lambda a, h, i: held.at[a, h, i], array, half)
                    ring = second[half]
                out.append(
                    Gather(ring, block, send.at[array, half, phase], recv.at[array, half, phase])
                )
        return out

    for array, ref in ((1, cots_ref), (0, rows_ref)):
        for half in (0, 1):
            held[array, half, second[half].place, first[half].place] = ref[
                half * rows : (half + 1) * rows, :
            ]
    near_gathers, far_gathers = gathers(0), gathers(1)
    for g in near_gathers:
        g.start()
    for g in near_gathers:
        g.before()
        g.after()
    for g, h in zip(near_gathers, far_gathers):
        g.across()
        h.start()

    def reduces(array, phase):
        out = []
        for half in (0, 1):
            if phase == 0:
                part = functools.partial(lambda h, i: parts.at[array, h, i], half)
                ring, boxes = second[half], (far.at[array, half], near.at[array, half])
            else:
                part = functools.partial(lambda h, i: own2.at[array, h, i], half)
                ring, boxes = first[half], (far2.at[array, half], near2.at[array, half])
            out.append(
                Reduce(
                    ring,
                    part,
                    *boxes,
                    send.at[array, half, 2 + phase],
                    recv.at[array, half, 2 + phase],
                )
            )
        return out

    both = SIDE * rows

    def group(k, carried):
        @pl.when(k == 1)
        def _():
            for g in far_gathers:
                g.before()

        @pl.when(k == 2)
        def _():
            for g in far_gathers:
                g.after()

        @pl.when(k == 3)
        def _():
            for g in far_gathers:
                g.across()

        shift = jnp.where(k == 0, 0, jnp.where(k == 1, SIDE - 1, jnp.where(k == 2, 1, 2)))
        places = [(second[h].place + shift) % SIDE for h in (0, 1)]

        def taken(array):
            return jnp.concatenate(
                [held[array, h, places[h]].reshape(both, width) for h in (0, 1)], axis=0
            )

        def put(array, tile, value):
            value = value.astype(bf16)
            for h in (0, 1):
                parts[array, h, places[h], :, :, tile] = value[
                    h * both : (h + 1) * both
                ].reshape(SIDE, rows, -1)

        x = taken(0)
        gate = jnp.dot(x, wg_ref[...], preferred_element_type=f32)
        up = jnp.dot(x, wu_ref[...], preferred_element_type=f32)
        hidden_grad = contract_last(taken(1), wd_ref[...])
        sigma = 1.0 / (1.0 + jnp.exp(-gate))
        active = gate * sigma
        hidden = (active * up).astype(bf16)
        gate_grad = (hidden_grad * up * sigma * (1.0 + gate * (1.0 - sigma))).astype(bf16)
        up_grad = (hidden_grad * active).astype(bf16)
        step = 512
        for n in range(width // step):
            tile = slice(n * step, (n + 1) * step)
            put(
                1,
                tile,
                contract_last(gate_grad, wg_ref[tile, :]) + contract_last(up_grad, wu_ref[tile, :]),
            )

        @pl.when(k == 3)
        def _():
            for r in reduces(1, 0):
                r.start()

        for n in range(width // step):
            tile = slice(n * step, (n + 1) * step)
            put(0, tile, jnp.dot(hidden, wd_ref[:, tile], preferred_element_type=f32))
        return carried

    lax.fori_loop(0, SIDE, group, 0)
    grads, outs = reduces(1, 0), reduces(0, 0)
    grads2, outs2 = reduces(1, 1), reduces(0, 1)
    for r in grads:
        r.middle()
    for r in outs:
        r.start()
    for half in (0, 1):
        own2[1, half] = grads[half].total()
        grads2[half].start()
    for r in outs:
        r.middle()
    for r in grads2:
        r.middle()
    for half in (0, 1):
        grad_ref[half * rows : (half + 1) * rows, :] = grads2[half].total()
    for half in (0, 1):
        own2[0, half] = outs[half].total()
        outs2[half].start()
    for r in outs2:
        r.middle()
    for half in (0, 1):
        out_ref[half * rows : (half + 1) * rows, :] = outs2[half].total()
    for g in near_gathers + far_gathers:
        g.finish()
    for r in grads + outs + grads2 + outs2:
        r.finish()


def experts(rows, cots, w_gate, w_up, w_down):
    count, width = rows.shape
    half = count // 2
    bf16 = jnp.bfloat16
    full = pltpu.VMEM((2, 2, SIDE, SIDE, half, width), bf16)
    return pl.pallas_call(
        experts_kernel,
        out_shape=[jax.ShapeDtypeStruct((count, width), bf16)] * 2,
        in_specs=[VMEM] * 5,
        out_specs=[VMEM] * 2,
        scratch_shapes=[
            full,
            full,
            pltpu.VMEM((2, 2, 2, SIDE // 2, half, width), bf16),
            pltpu.VMEM((2, 2, 2, SIDE, half, width), bf16),
            pltpu.VMEM((2, 2, SIDE, half, width), bf16),
            pltpu.VMEM((2, 2, 2, half // 2, width), bf16),
            pltpu.VMEM((2, 2, 2, half, width), bf16),
            pltpu.SemaphoreType.DMA((2, 2, 4, 4)),
            pltpu.SemaphoreType.DMA((2, 2, 4, 4)),
        ],
        compiler_params=pltpu.CompilerParams(
            vmem_limit_bytes=58 * 1024 * 1024, collective_id=1, has_side_effects=True
        ),
    )(rows, cots, w_gate, w_up, w_down)


def entering(ends, sums, rate2, backward):
    count = sums.shape[0]
    place = lax.axis_index("ctx")
    index = jnp.arange(count)
    if backward:
        between = (index[None, :] > place) & (index[None, :] < index[:, None])
        live = index > place
    else:
        between = (index[None, :] < place) & (index[None, :] > index[:, None])
        live = index < place
    gap = jnp.sum(jnp.where(between[:, :, None], sums[None], 0.0), axis=1)
    terms = jnp.exp2(gap[:, None, :] * rate2[None]) * ends.astype(jnp.float32)
    return jnp.sum(jnp.where(live[:, None, None], terms, 0.0), axis=0)


def local(
    u_in,
    z_gate,
    delta,
    b_in,
    c_in,
    rate,
    skip,
    w_out,
    resid,
    gain,
    expert_ids,
    route_weights,
    w_gate,
    w_up,
    w_down,
    d_out,
):
    seg_rows, channels = u_in.shape
    states = rate.shape[0]
    my_rows, width = resid.shape
    experts_count = lax.axis_size("exp")
    capacity = 4 * my_rows // experts_count
    f32 = jnp.float32
    shape = jax.ShapeDtypeStruct
    plane = pltpu.VMEM((seg_rows, channels), f32)
    rate2 = rate * (-math.log2(math.e))
    skip_row = skip[None, :]
    brep = jnp.broadcast_to(b_in[:, :, None], (seg_rows, states, LANES))
    crep = jnp.broadcast_to(c_in[:, :, None], (seg_rows, states, LANES))
    z_act = jax.nn.silu(z_gate.astype(f32))
    state_end, last_sum = local_call(
        forward_end,
        [shape((states, channels), f32), shape((1, channels), f32)],
        [plane],
        (delta, u_in, brep, rate2),
    )
    sums = lax.all_gather(last_sum[0], "ctx")
    ends = lax.all_gather(state_end.astype(jnp.bfloat16), "ctx")
    state_in = entering(ends, sums, rate2, False)
    (gated,) = local_call(
        forward_out,
        [shape((seg_rows, channels), jnp.bfloat16)],
        [plane, plane],
        (delta, u_in, brep, crep, rate2, state_in, skip_row, z_gate),
    )
    mixed = lax.psum_scatter(
        jnp.dot(gated, w_out, preferred_element_type=jnp.float32).astype(jnp.bfloat16),
        "exp",
        scatter_dimension=0,
        tiled=True,
    ).astype(jnp.float32)
    stream = resid.astype(jnp.float32) + mixed
    inverse = lax.rsqrt(jnp.mean(stream * stream, axis=-1, keepdims=True) + 1e-05)
    normed = (stream * inverse * gain[None, :]).astype(jnp.bfloat16)
    owners = expert_ids.reshape(-1)
    assign_count = owners.shape[0]
    onehot = (owners[:, None] == jnp.arange(experts_count, dtype=jnp.int32)[None, :]).astype(
        jnp.float32
    )
    assign_index = jnp.arange(assign_count)
    strict = (assign_index[:, None] > assign_index[None, :]).astype(jnp.float32)
    before = jnp.dot(strict, onehot, precision=lax.Precision.HIGHEST)
    slots = jnp.sum(before * onehot, axis=1).astype(jnp.int32)
    target = owners * capacity + slots
    placing = (
        jnp.arange(experts_count * capacity, dtype=jnp.int32)[:, None] == target[None, :]
    ).astype(jnp.bfloat16)
    paired = jnp.repeat(normed, 2, axis=0)
    outgoing = (
        jnp.dot(placing, paired, preferred_element_type=jnp.float32)
        .astype(jnp.bfloat16)
        .reshape(experts_count, capacity, width)
    )
    cotangent = (
        route_weights.reshape(-1)[:, None] * jnp.repeat(d_out.astype(jnp.float32), 2, axis=0)
    ).astype(jnp.bfloat16)
    grad_outgoing = (
        jnp.dot(placing, cotangent, preferred_element_type=jnp.float32)
        .astype(jnp.bfloat16)
        .reshape(experts_count, capacity, width)
    )
    arrived = lax.all_to_all(outgoing, "exp", split_axis=0, concat_axis=0, tiled=True)
    grad_arrived = lax.all_to_all(grad_outgoing, "exp", split_axis=0, concat_axis=0, tiled=True)
    summed, row_sums = experts(
        arrived.reshape(-1, width), grad_arrived.reshape(-1, width), w_gate[0], w_up[0], w_down[0]
    )
    row_sums = row_sums.reshape(arrived.shape)
    summed = summed.reshape(arrived.shape)
    returned = lax.all_to_all(summed, "exp", split_axis=0, concat_axis=0, tiled=True)
    expert_out = lax.dot_general(
        placing,
        returned.reshape(-1, width),
        (((0,), (0,)), ((), ())),
        preferred_element_type=jnp.float32,
    )
    expert_out = expert_out.reshape(my_rows, 2, width)
    final = (
        stream + route_weights[:, 0:1] * expert_out[:, 0] + route_weights[:, 1:2] * expert_out[:, 1]
    ).astype(jnp.bfloat16)
    grad_back = lax.all_to_all(row_sums, "exp", split_axis=0, concat_axis=0, tiled=True)
    normed_grad = lax.dot_general(
        placing,
        grad_back.reshape(-1, width),
        (((0,), (0,)), ((), ())),
        preferred_element_type=jnp.float32,
    )
    normed_grad = normed_grad.reshape(my_rows, 2, width)
    normed_grad = normed_grad[:, 0] + normed_grad[:, 1]
    scaled = normed_grad * gain[None, :]
    project_mean = jnp.mean(scaled * stream, axis=-1, keepdims=True)
    stream_grad = inverse * (scaled - stream * inverse * inverse * project_mean)
    grad_resid = (d_out.astype(jnp.float32) + stream_grad).astype(jnp.bfloat16)
    segment_grad = lax.all_gather(grad_resid, "exp", axis=0, tiled=True)
    out_grad = contract_last(segment_grad, w_out) * z_act
    (back_end,) = local_call(
        backward_end,
        [shape((states, channels), f32)],
        [],
        (delta, out_grad, crep, rate2),
    )
    back_ends = lax.all_gather(back_end.astype(jnp.bfloat16), "ctx")
    grad_in = entering(back_ends, sums, rate2, True)
    (grad_u,) = local_call(
        backward_out,
        [shape((seg_rows, channels), jnp.bfloat16)],
        [plane],
        (delta, out_grad, brep, crep, rate2, grad_in, skip_row),
    )
    return (final, grad_resid, grad_u)


def solution(mesh):
    return jax.shard_map(
        local,
        mesh=mesh,
        in_specs=(
            P("ctx", "exp"),
            P("ctx", "exp"),
            P("ctx", "exp"),
            P("ctx", None),
            P("ctx", None),
            P(None, "exp"),
            P("exp"),
            P("exp", None),
            P(("ctx", "exp"), None),
            P(),
            P(("ctx", "exp"), None),
            P(("ctx", "exp"), None),
            P("exp", None, "ctx"),
            P("exp", None, "ctx"),
            P("exp", "ctx", None),
            P(("ctx", "exp"), None),
        ),
        out_specs=(P(("ctx", "exp"), None), P(("ctx", "exp"), None), P("ctx", "exp")),
        check_vma=False,
    )
```

time: 745 us -> 372 us (0.50)
  waiting for transfers between devices: 303 us -> 108 us
  other arithmetic: 146 us -> 7.09 us
  Pallas kernels: 0 us -> 118 us
  local copies, waits for them, and re-layouts: 97.4 us -> 14 us
  blocking collectives: 109 us -> 57.2 us
  matrix products: 41.3 us -> 7.6 us
  starting transfers between devices: 17.8 us -> 40.3 us
    pallas_call x0 -> x5, Pallas kernels: none -> 118 us  [the longest x1 107 us: experts(): pl.pallas_call(experts_kernel, out_shape=[jax.ShapeDtypeStruct((count, wi...]
    reduce_sum x66 -> x0, other arithmetic: 106 us -> none  [the longest x16 46 us: forward_advance(): inner = jnp.sum(weight * source[None], axis=1)]
    unnamed x7 -> x2, waiting for transfers between devices: 103 us -> 0.03 us
    reduce_scatter x1 -> x0, waiting for transfers between devices: 62.9 us -> none  [local(): lax.psum_scatter(partial_out.astype(jnp.bfloat16), 'ctx', scatter_dimensi...]
    all_to_all x2 -> x0, blocking collectives: 51.5 us -> none  [the longest x1 32 us: local(): lax.all_to_all(grad_outgoing, 'exp', split_axis=0, concat_axis=0, tiled=T...]
    mul x64 -> x0, local copies, waits for them, and re-layouts: 47.5 us -> none  [the longest x16 12.2 us: forward_advance(): source = b_rows[:, :, None] * drv[:, None, :]]
    all_gather x2 -> x0, waiting for transfers between devices: 42.5 us -> none  [the longest x1 42.4 us: local(): every_rows = lax.all_gather(arrived, 'ctx', axis=0, tiled=True)]
    all_to_all x0 -> x2, starting transfers between devices: none -> 28.2 us  [the longest x1 20 us: local(): lax.all_to_all(grad_outgoing, 'exp', split_axis=0, concat_axis=0, tiled=T...]
  transfers between devices with their start and end apart: 8 -> 6, of which waited for: 7 -> 5; matrix products, arithmetic and copies ran while one was open for 5% -> 3% of each run, Pallas kernels for 0% -> 0%
where the time goes in v1:
time: 372 us; the launch traced here: 367 us
  Pallas kernels  118 us (32%)
  waiting for transfers between devices  108 us (29%)
  blocking collectives  57.2 us (15%)
  starting transfers between devices  40.3 us (11%)
  between operations  14.4 us (4%)
  local copies, waits for them, and re-layouts  14 us (4%)
  matrix products  7.6 us (2%)
  other arithmetic  7.09 us (2%)
    pallas_call x1, Pallas kernels, experts(): pl.pallas_call(experts_kernel, out_shape=[jax.ShapeDtypeStruct((count, wi...  107 us
    reduce_scatter x1, waiting for transfers between devices, local(): lax.psum_scatter(jnp.dot(gated, w_out, preferred_element_type=jnp.float32...  45.9 us
    all_gather x1, waiting for transfers between devices, local(): segment_grad = lax.all_gather(grad_resid, 'exp', axis=0, tiled=True)  33.4 us
    all_gather x1, blocking collectives, local(): ends = lax.all_gather(state_end.astype(jnp.bfloat16), 'ctx')  21.7 us
    all_to_all x1, starting transfers between devices, local(): lax.all_to_all(grad_outgoing, 'exp', split_axis=0, concat_axis=0, tiled=T...  20 us
    all_gather x1, blocking collectives, local(): back_ends = lax.all_gather(back_end.astype(jnp.bfloat16), 'ctx')  18.5 us
    all_gather x1, blocking collectives, local(): sums = lax.all_gather(last_sum[0], 'ctx')  17 us
    pallas_call x4, Pallas kernels, local_call(): pl.pallas_call(body, out_shape=outs, in_specs=[VMEM] * len(args), out_spe...  11.2 us
  transfers between devices with their start and end apart: 6, of which 5 were waited for; matrix products, arithmetic and copies ran while one was open for 3% of the time, Pallas kernels for 0%

profile of v1, /device:TPU:1, one launch (start us, length us, event | category | flops | bytes accessed | tf_op | source)
XLA Modules:
  0.0 367.2 jit_solution(5961570197839235244)
XLA Ops:
  7.2 1.0 copy.29
  8.2 0.8 copy.30
  10.4 1.8 shard_map.175
  12.2 1.3 copy-done.1
  13.5 21.7 %all-gather = bf16[256,512]{1,0:T(8,128)(2,1)} all-gather(bf16[16,512]{1,0:T(8,128)(2,1)S(1)} %convert_element_type.57), channel_id=2, replica_groups=mesh['ctx'=16,'exp'=16] {'ctx'}, dimensions={0}, use_global_device_ids=true | all-gather | bytes 278528 | tf_op jit(solution)/shard_map/all_gather | solution.py:526
  35.2 17.0 %all-gather.2 = f32[16,1,512]{2,1,0:T(1,128)S(1)} all-gather(f32[1,1,512]{2,1,0:T(1,128)S(1)} %bitcast.49), channel_id=1, replica_groups=mesh['ctx'=16,'exp'=16] {'ctx'}, dimensions={0}, use_global_device_ids=true | all-gather | bytes 34816 | tf_op jit(solution)/shard_map/all_gather | solution.py:525
  52.3 1.4 fusion.43.start_ref
  54.3 3.6 shard_map.176
  57.9 1.7 convolution_convert_fusion
  61.6 20.0 %all-to-all-start.1 = ((bf16[16,4,2048]{2,1,0:T(4,128)(2,1)}), bf16[16,4,2048]{2,1,0:T(4,128)(2,1)S(1)}, u32[]{:S(2)}, u32[]{:S(2)}) async-start(bf16[16,4,2048]{2,1,0:T(4,128)(2,1)} %reshape.183), calls=%async_computation.2 | async-start | bytes 524288 | tf_op jit(solution)/shard_map/all_to_all | solution.py:571
  81.6 45.9 %reduce-scatter.2.cloned.1.call-done = bf16[16,2048]{1,0:T(8,128)(2,1)} async-done(((bf16[256,2048]{1,0:T(8,128)(2,1)}), bf16[16,2048]{1,0:T(8,128)(2,1)}) %reduce-scatter.2.cloned.1.call-update) | async-done | bytes 65552 | tf_op jit(solution)/shard_map/reduce_scatter | solution.py:534
  127.5 1.0 multiply_reduce_fusion.1
  128.5 0.9 multiply_convert_fusion.2
  130.2 1.1 convolution_convert_fusion.2
  132.1 8.1 %all-to-all-start = ((bf16[16,4,2048]{2,1,0:T(4,128)(2,1)}), bf16[16,4,2048]{2,1,0:T(4,128)(2,1)S(1)}, u32[]{:S(2)}, u32[]{:S(2)}) async-start(bf16[16,4,2048]{2,1,0:T(4,128)(2,1)} %reshape.180), calls=%async_computation.1 | async-start | bytes 524288 | tf_op jit(solution)/shard_map/all_to_all | solution.py:570
  141.0 10.9 %all-to-all-done = bf16[16,4,2048]{2,1,0:T(4,128)(2,1)S(1)} async-done(((bf16[16,4,2048]{2,1,0:T(4,128)(2,1)}), bf16[16,4,2048]{2,1,0:T(4,128)(2,1)S(1)}, u32[]{:S(2)}, u32[]{:S(2)}) %all-to-all-start) | async-done | bytes 262176 | tf_op jit(solution)/shard_map/all_to_all | solution.py:570
  152.7 107.1 %shard_map.177 = (bf16[64,2048]{1,0:T(8,128)(2,1)}, bf16[64,2048]{1,0:T(8,128)(2,1)}) custom-call(bf16[64,2048]{1,0:T(8,128)(2,1)} %reshape.181.rows_ref, bf16[64,2048]{1,0:T(8,128)(2,1)} %reshape.184.cots_ref, bf16[2048,512]{1,0:T(8,128)(2,1)} %bitcast.50, bf16[2048,512]{1,0:T(8,128)(2,1)} %bitcast.51, bf16[512,2048]{1,0:T(8,128)(2,1)} %bitcast.52), custom_call_target="tpu_custom_call" | custom-call | tf_op jit(solution)/shard_map/pallas_call | solution.py:451
  259.8 1.8 reshape.187
  261.5 8.7 %all-to-all-start.3 = ((bf16[16,4,2048]{2,1,0:T(4,128)(2,1)}), bf16[16,4,2048]{2,1,0:T(4,128)(2,1)S(1)}, u32[]{:S(2)}, u32[]{:S(2)}) async-start(bf16[16,4,2048]{2,1,0:T(4,128)(2,1)} %reshape.187), calls=%async_computation.4 | async-start | bytes 524288 | tf_op jit(solution)/shard_map/all_to_all | solution.py:588
  270.3 1.8 reshape.185
  272.1 10.0 %all-to-all-done.3 = bf16[16,4,2048]{2,1,0:T(4,128)(2,1)S(1)} async-done(((bf16[16,4,2048]{2,1,0:T(4,128)(2,1)}), bf16[16,4,2048]{2,1,0:T(4,128)(2,1)S(1)}, u32[]{:S(2)}, u32[]{:S(2)}) %all-to-all-start.3) | async-done | bytes 262176 | tf_op jit(solution)/shard_map/all_to_all | solution.py:588
  282.1 3.4 all-to-all-start.2
  286.3 1.1 fusion.36
  287.4 1.0 multiply_reduce_fusion
  288.4 8.1 %all-to-all-done.2 = bf16[16,4,2048]{2,1,0:T(4,128)(2,1)S(1)} async-done(((bf16[16,4,2048]{2,1,0:T(4,128)(2,1)}), bf16[16,4,2048]{2,1,0:T(4,128)(2,1)S(1)}, u32[]{:S(2)}, u32[]{:S(2)}) %all-to-all-start.2) | async-done | bytes 262176 | tf_op jit(solution)/shard_map/all_to_all | solution.py:577
  297.3 1.1 fusion.38
  298.4 1.6 add_convert_fusion
  300.1 33.4 %all-gather.5.cloned.1.call-done = bf16[256,2048]{1,0:T(8,128)(2,1)} async-done(((bf16[16,2048]{1,0:T(8,128)(2,1)}), bf16[256,2048]{1,0:T(8,128)(2,1)}) %all-gather.5.cloned.1.call-update) | async-done | bytes 1048592 | tf_op jit(solution)/shard_map/all_gather | solution.py:601
  333.5 2.1 convolution_multiply_fusion.grad_ref
  335.7 1.8 shard_map.178
  337.4 18.5 %all-gather.1 = bf16[256,512]{1,0:T(8,128)(2,1)S(1)} all-gather(bf16[16,512]{1,0:T(8,128)(2,1)S(1)} %convert_element_type.70), channel_id=3, replica_groups=mesh['ctx'=16,'exp'=16] {'ctx'}, dimensions={0}, use_global_device_ids=true | all-gather | bytes 278528 | tf_op jit(solution)/shard_map/all_gather | solution.py:609
  356.3 4.1 %shard_map.179 = bf16[256,512]{1,0:T(8,128)(2,1)} custom-call(f32[256,512]{1,0:T(8,128)S(1)} %copy-done.6, f32[256,512]{1,0:T(8,128)S(1)} %convolution_multiply_fusion.grad_ref, f32[256,16,128]{2,1,0:T(8,128)S(1)} %copy-done.3, f32[256,16,128]{2,1,0:T(8,128)S(1)} %copy-done.5, f32[16,512]{1,0:T(8,128)S(1)} %broadcast_multiply_fusion.rate_ref, ...), custom_call_target="tpu_custom_call" | custom-call | tf_op jit(solution)/shard_map/pallas_call | solution.py:136
  (71 shorter events, 9.1 us)
Async XLA Ops:
  7.2 50.7 %copy-start = (bf16[512,2048]{1,0:T(8,128)(2,1)S(1)}, bf16[512,2048]{1,0:T(8,128)(2,1)}, u32[]{:S(2)}) copy-start(bf16[512,2048]{1,0:T(8,128)(2,1)} %param.23) | copy-start | bytes 6291460
  7.2 3.2 copy-start.6
  7.2 3.2 copy-start.7
  7.2 120.3 %reduce-scatter.2.cloned.1.call-start = ((), (), s32[]{:S(2)}) async-start(), calls=%async_computation.5 | async-start | bytes 1114112 | tf_op jit(solution)/shard_map/reduce_scatter | solution.py:534
  12.2 1.3 copy-start.1
  13.5 40.7 %copy-start.8 = (bf16[256,512]{1,0:T(8,128)(2,1)S(1)}, bf16[256,512]{1,0:T(8,128)(2,1)}, u32[]{:S(2)}) copy-start(bf16[256,512]{1,0:T(8,128)(2,1)} %z_ref.1) | copy-start | bytes 786436
  13.5 40.7 %copy-start.9 = (f32[512]{0:T(512)S(1)}, f32[512]{0:T(512)}, u32[]{:S(2)}) copy-start(f32[512]{0:T(512)} %param.22) | copy-start | bytes 6148
  52.2 5.6 %copy-start.13 = (f32[16,1,512]{2,0,1:T(8,128)}, f32[16,1,512]{2,0,1:T(8,128)S(1)}, u32[]{:S(2)}) copy-start(f32[16,1,512]{2,0,1:T(8,128)S(1)} %copy.41) | copy-start | bytes 98308
  52.2 2.1 copy-start.2
  54.3 3.6 copy-start.4
  57.9 1.8 copy-start.16
  57.9 2.0 copy-start.11
  57.9 2.3 copy-start.15
  59.6 67.8 %copy-start.10 = (bf16[16,2048]{1,0:T(8,128)(2,1)S(1)}, bf16[16,2048]{1,0:T(8,128)(2,1)}, u32[]{:S(2)}) copy-start(bf16[16,2048]{1,0:T(8,128)(2,1)} %param.24) | copy-start | bytes 196612
  59.6 68.8 %copy-start.12 = (f32[2048]{0:T(1024)S(1)}, f32[2048]{0:T(1024)}, u32[]{:S(2)}) copy-start(f32[2048]{0:T(1024)} %param.25) | copy-start | bytes 24580
  61.6 70.5 %all-to-all-start.1 = ((bf16[16,4,2048]{2,1,0:T(4,128)(2,1)}), bf16[16,4,2048]{2,1,0:T(4,128)(2,1)S(1)}, u32[]{:S(2)}, u32[]{:S(2)}) async-start(bf16[16,4,2048]{2,1,0:T(4,128)(2,1)} %reshape.183), calls=%async_computation.2 | async-start | bytes 524288 | tf_op jit(solution)/shard_map/all_to_all | solution.py:571
  132.1 19.9 %all-to-all-start = ((bf16[16,4,2048]{2,1,0:T(4,128)(2,1)}), bf16[16,4,2048]{2,1,0:T(4,128)(2,1)S(1)}, u32[]{:S(2)}, u32[]{:S(2)}) async-start(bf16[16,4,2048]{2,1,0:T(4,128)(2,1)} %reshape.180), calls=%async_computation.1 | async-start | bytes 524288 | tf_op jit(solution)/shard_map/all_to_all | solution.py:570
  261.5 20.5 %all-to-all-start.3 = ((bf16[16,4,2048]{2,1,0:T(4,128)(2,1)}), bf16[16,4,2048]{2,1,0:T(4,128)(2,1)S(1)}, u32[]{:S(2)}, u32[]{:S(2)}) async-start(bf16[16,4,2048]{2,1,0:T(4,128)(2,1)} %reshape.187), calls=%async_computation.4 | async-start | bytes 524288 | tf_op jit(solution)/shard_map/all_to_all | solution.py:588
  282.1 14.5 %all-to-all-start.2 = ((bf16[16,4,2048]{2,1,0:T(4,128)(2,1)}), bf16[16,4,2048]{2,1,0:T(4,128)(2,1)S(1)}, u32[]{:S(2)}, u32[]{:S(2)}) async-start(bf16[16,4,2048]{2,1,0:T(4,128)(2,1)} %reshape.185), calls=%async_computation.3 | async-start | bytes 524288 | tf_op jit(solution)/shard_map/all_to_all | solution.py:577
  285.5 48.0 %all-gather.5.cloned.1.call-start = ((), (), s32[]{:S(2)}) async-start(), calls=%async_computation.6 | async-start | bytes 1114112 | tf_op jit(solution)/shard_map/all_gather | solution.py:601
  333.5 2.1 copy-start.5
  335.6 20.3 %copy-start.14 = (f32[16,1,512]{2,0,1:T(8,128)S(1)}, f32[16,1,512]{2,0,1:T(8,128)}, u32[]{:S(2)}) copy-start(f32[16,1,512]{2,0,1:T(8,128)} %copy-done.13) | copy-start | bytes 98308
  335.7 20.6 %copy-start.3 = (f32[256,16,128]{2,1,0:T(8,128)S(1)}, f32[256,16,128]{2,1,0:T(8,128)}, u32[]{:S(2)}) copy-start(f32[256,16,128]{2,1,0:T(8,128)} %copy-done.1) | copy-start | bytes 6291460
Sparse Core Ops, SparseCore 0:
  59.8 67.6 reduce-scatter.1
  300.2 33.2 all-gather.4

commit v2 on v1

v2 whole, which is shorter than its diff:
```python
import functools
import math

import jax
import jax.numpy as jnp
from jax import lax
from jax.experimental import pallas as pl
from jax.experimental.pallas import tpu as pltpu
from jax.sharding import PartitionSpec as P

LANES = 128
VMEM = pl.BlockSpec(memory_space=pltpu.VMEM)


def contract_last(left, right):
    return lax.dot_general(
        left, right, (((1,), (1,)), ((), ())), preferred_element_type=jnp.float32
    )


def silu(v):
    return v * (1.0 / (1.0 + jnp.exp(-v)))


def tiles_of(channels):
    return [slice(i * LANES, (i + 1) * LANES) for i in range(channels // LANES)]


GROUP = 8


def scan_tokens(rows, channels, planes, step, initial, out_ref=None, backward=False):
    tiles = tiles_of(channels)
    row_index = lax.broadcasted_iota(jnp.int32, (GROUP, LANES), 0)

    def group(i, carried):
        base = rows - GROUP - i * GROUP if backward else i * GROUP
        base = pl.multiple_of(base, GROUP)
        blocks = [[plane[pl.ds(base, GROUP), tile] for plane in planes] for tile in tiles]
        made = [jnp.zeros((GROUP, LANES), jnp.float32) for _ in tiles]
        carried = list(carried)
        for j in reversed(range(GROUP)) if backward else range(GROUP):
            for k, tile in enumerate(tiles):
                line = [b[j : j + 1] for b in blocks[k]]
                carried[k], row = step(base + j, tile, line, carried[k])
                if out_ref is not None:
                    made[k] = jnp.where(row_index == j, row, made[k])
        if out_ref is not None:
            for k, tile in enumerate(tiles):
                out_ref[pl.ds(base, GROUP), tile] = made[k]
        return tuple(carried)

    return lax.fori_loop(0, rows // GROUP, group, tuple(initial))


def zero_state(rate_ref):
    states, channels = rate_ref.shape
    return [jnp.zeros((states, LANES), jnp.float32) for _ in tiles_of(channels)]


SIDE = 4
TO_RIGHT, TO_LEFT, ON_RIGHT, ON_LEFT = 0, 1, 2, 3


class Ring:
    def __init__(self, along_x):
        c = lax.axis_index("ctx")
        x, y = c // SIDE, c % SIDE
        self.place = x if along_x else y
        up, down = (self.place + 1) % SIDE, (self.place + SIDE - 1) % SIDE
        self.after, self.before, self.across = up, down, (self.place + 2) % SIDE
        self.right = {"ctx": up * SIDE + y if along_x else x * SIDE + up}
        self.left = {"ctx": down * SIDE + y if along_x else x * SIDE + down}


def halves(ref):
    n = ref.shape[0] // 2
    return ref.at[pl.ds(0, n)], ref.at[pl.ds(n, n)]


class Gather:
    def __init__(self, ring, block, send, recv):
        self.ring, self.block, self.send, self.recv = ring, block, send, recv

    def copy(self, ref, way):
        target = self.ring.right if way in (TO_RIGHT, ON_RIGHT) else self.ring.left
        return pltpu.make_async_remote_copy(
            src_ref=ref,
            dst_ref=ref,
            send_sem=self.send.at[way],
            recv_sem=self.recv.at[way],
            device_id=target,
            device_id_type=pl.DeviceIdType.MESH,
        )

    def start(self):
        own = self.block(self.ring.place)
        self.copy(own, TO_RIGHT).start()
        self.copy(own, TO_LEFT).start()

    def before(self):
        came = self.block(self.ring.before)
        self.copy(came, TO_RIGHT).wait_recv()
        self.copy(halves(came)[0], ON_RIGHT).start()

    def after(self):
        came = self.block(self.ring.after)
        self.copy(came, TO_LEFT).wait_recv()
        self.copy(halves(came)[1], ON_LEFT).start()

    def across(self):
        first, second = halves(self.block(self.ring.across))
        self.copy(first, ON_RIGHT).wait_recv()
        self.copy(second, ON_LEFT).wait_recv()

    def finish(self):
        own = self.block(self.ring.place)
        self.copy(own, TO_RIGHT).wait_send()
        self.copy(own, TO_LEFT).wait_send()
        self.copy(halves(self.block(self.ring.before))[0], ON_RIGHT).wait_send()
        self.copy(halves(self.block(self.ring.after))[1], ON_LEFT).wait_send()


def add_into(total, term):
    total[...] = (total[...].astype(jnp.float32) + term[...].astype(jnp.float32)).astype(
        total.dtype
    )


class Reduce:
    def __init__(self, ring, part, far, near, send, recv):
        self.ring, self.part, self.far, self.near = ring, part, far, near
        self.send, self.recv = send, recv

    def copy(self, way):
        ring = self.ring
        source = {
            TO_RIGHT: lambda: halves(self.part(ring.across))[0],
            TO_LEFT: lambda: halves(self.part(ring.across))[1],
            ON_RIGHT: lambda: self.part(ring.after),
            ON_LEFT: lambda: self.part(ring.before),
        }[way]()
        target = {
            TO_RIGHT: self.far.at[0],
            TO_LEFT: self.far.at[1],
            ON_RIGHT: self.near.at[0],
            ON_LEFT: self.near.at[1],
        }[way]
        return pltpu.make_async_remote_copy(
            src_ref=source,
            dst_ref=target,
            send_sem=self.send.at[way],
            recv_sem=self.recv.at[way],
            device_id=ring.right if way in (TO_RIGHT, ON_RIGHT) else ring.left,
            device_id_type=pl.DeviceIdType.MESH,
        )

    def start(self):
        self.copy(TO_RIGHT).start()
        self.copy(TO_LEFT).start()

    def middle(self):
        self.copy(TO_RIGHT).wait_recv()
        add_into(halves(self.part(self.ring.after))[0], self.far.at[0])
        self.copy(ON_RIGHT).start()
        self.copy(TO_LEFT).wait_recv()
        add_into(halves(self.part(self.ring.before))[1], self.far.at[1])
        self.copy(ON_LEFT).start()

    def total(self):
        self.copy(ON_RIGHT).wait_recv()
        self.copy(ON_LEFT).wait_recv()
        f32 = jnp.float32
        own = self.part(self.ring.place)
        return (
            own[...].astype(f32) + self.near[0].astype(f32) + self.near[1].astype(f32)
        ).astype(own.dtype)

    def finish(self):
        for way in range(4):
            self.copy(way).wait_send()


def barrier_with(axes):
    barrier = pltpu.get_barrier_semaphore()
    total = 0
    for axis in axes:
        count = lax.axis_size(axis)
        me = lax.axis_index(axis)

        def signal(d, carried):
            pl.semaphore_signal(
                barrier,
                inc=1,
                device_id={axis: (me + d) % count},
                device_id_type=pl.DeviceIdType.MESH,
            )
            return carried

        lax.fori_loop(1, count, signal, 0)
        total += count - 1
    pl.semaphore_wait(barrier, total)


def remote(source, target, send, recv, device):
    return pltpu.make_async_remote_copy(
        src_ref=source,
        dst_ref=target,
        send_sem=send,
        recv_sem=recv,
        device_id=device,
        device_id_type=pl.DeviceIdType.MESH,
    )


def each(low, high, body):
    def step(i, carried):
        body(i)
        return carried

    lax.fori_loop(low, high, step, 0)


class Exchange:
    def __init__(self, source, box, send, recv):
        self.source, self.box, self.send, self.recv = source, box, send, recv
        self.me, self.count = lax.axis_index("exp"), lax.axis_size("exp")

    def copy(self, other, slot):
        return remote(
            self.source.at[other],
            self.box.at[slot],
            self.send.at[other],
            self.recv.at[slot],
            {"exp": other},
        )

    def start(self):
        self.box[self.me] = self.source[self.me]
        each(1, self.count, lambda d: self.copy((self.me + d) % self.count, self.me).start())

    def wait(self):
        def one(d):
            other = (self.me + d) % self.count
            self.copy(other, other).wait_recv()

        each(1, self.count, one)

    def finish(self):
        each(1, self.count, lambda d: self.copy((self.me + d) % self.count, self.me).wait_send())


class Spread:
    def __init__(self, source, box, send, recv):
        self.source, self.box, self.send, self.recv = source, box, send, recv
        self.me = lax.axis_index("ctx")

    def copy(self, other, slot):
        return remote(
            self.source,
            self.box.at[slot],
            self.send.at[other],
            self.recv.at[slot],
            {"ctx": other},
        )

    def start(self, low, high):
        each(low, high, lambda other: self.copy(other, self.me).start())

    def wait_one(self, other):
        self.copy(other, other).wait_recv()

    def finish(self, low, high):
        each(low, high, lambda other: self.copy(other, self.me).wait_send())


def regroup(quarter, rows, slots, transposed):
    size = (rows * 4, rows) if transposed else (rows, rows * 4)
    row = lax.broadcasted_iota(jnp.int32, size, 1 if transposed else 0)
    slab = lax.broadcasted_iota(jnp.int32, size, 0 if transposed else 1)
    place = (row // slots) * (4 * slots) + quarter * slots + row % slots
    return jnp.where(slab == place, 1.0, 0.0).astype(jnp.bfloat16)


def quarters(value):
    step = value.shape[-1] // 4
    return jnp.concatenate([value[:, q * step : (q + 1) * step] for q in range(4)], axis=0)


def whole(value):
    step = value.shape[0] // 4
    return jnp.concatenate([value[q * step : (q + 1) * step] for q in range(4)], axis=1)


def layer_kernel(
    delta_ref,
    u_ref,
    z_ref,
    brep_ref,
    crep_ref,
    rate_ref,
    skip_ref,
    wout_ref,
    resid_ref,
    gain_ref,
    weight_ref,
    place_ref,
    placet_ref,
    wg_ref,
    wu_ref,
    wd_ref,
    dout_ref,
    final_ref,
    gresid_ref,
    gradu_ref,
    drive,
    y,
    gated,
    end16,
    back16,
    sums,
    end_box,
    sum_box,
    back_box,
    state_send,
    state_recv,
    mixed,
    pair_box,
    mix_box,
    mix_send,
    mix_recv,
    slabs,
    boxes,
    slab_send,
    slab_recv,
    stream,
    segment,
    seg_send,
    seg_recv,
    held,
    parts,
    far,
    near,
    own2,
    far2,
    near2,
    send,
    recv,
):
    f32 = jnp.float32
    bf16 = jnp.bfloat16
    ring_x, ring_y = Ring(True), Ring(False)
    first = (ring_x, ring_y)
    second = (ring_y, ring_x)
    rows, width = held.shape[-2], held.shape[-1]
    seg_rows, channels = delta_ref.shape
    ctx, ctx_count = lax.axis_index("ctx"), lax.axis_size("ctx")
    exp, exp_count = lax.axis_index("exp"), lax.axis_size("exp")
    z, core = exp // 2, exp % 2
    z_count = exp_count // 2
    sibling = {"exp": z * 2 + 1 - core}
    slots = 2 * rows // exp_count
    my_rows = resid_ref.shape[0]
    slab_rows = slabs.shape[2]
    slab_width = slabs.shape[3]
    COT, ROW, GRAD, OUT = range(4)
    moves = [Exchange(slabs.at[i], boxes.at[i], slab_send.at[i], slab_recv.at[i]) for i in range(4)]
    ends = Spread(end16, end_box, state_send.at[0], state_recv.at[0])
    totals = Spread(sums, sum_box, state_send.at[1], state_recv.at[1])
    backs = Spread(back16, back_box, state_send.at[2], state_recv.at[2])

    def to_slabs(kind, value):
        slabs[kind] = value.astype(bf16).reshape(exp_count, slab_rows, slab_width)

    def dispatched(kind):
        flat = boxes[kind].reshape(exp_count * slab_rows, slab_width)
        return [
            jnp.dot(
                regroup(q, 2 * rows, slots, False), flat, preferred_element_type=f32
            ).astype(bf16)
            for q in range(4)
        ]

    def give_back(kind, read):
        total = None
        for q in range(4):
            tile = slice(q * slab_width, (q + 1) * slab_width)
            term = jnp.dot(
                regroup(q, 2 * rows, slots, True), read(tile), preferred_element_type=f32
            )
            total = term if total is None else total + term
        to_slabs(kind, total)

    def gather(array, half, phase):
        if phase == 0:
            block = lambda i: held.at[array, half, second[half].place, i]
            ring = first[half]
        else:
            block = lambda i: held.at[array, half, i]
            ring = second[half]
        return Gather(ring, block, send.at[array, half, phase], recv.at[array, half, phase])

    near_gathers = [[gather(a, h, 0) for h in (0, 1)] for a in (0, 1)]
    far_gathers = [[gather(a, h, 1) for h in (0, 1)] for a in (0, 1)]

    def take_in(array, kind):
        for q, value in enumerate(dispatched(kind)):
            tile = slice(q * slab_width, (q + 1) * slab_width)
            for half in (0, 1):
                held[array, half, second[half].place, first[half].place, :, tile] = value[
                    half * rows : (half + 1) * rows
                ]
        for g in near_gathers[array]:
            g.start()

    def spread_out(array):
        for g in near_gathers[array]:
            g.before()
            g.after()
        for g, h in zip(near_gathers[array], far_gathers[array]):
            g.across()
            h.start()

    def reduces(array, phase):
        out = []
        for half in (0, 1):
            if phase == 0:
                part = functools.partial(lambda h, i: parts.at[array, h, i], half)
                ring, inbox = second[half], (far.at[array, half], near.at[array, half])
            else:
                part = functools.partial(lambda h, i: own2.at[array, h, i], half)
                ring, inbox = first[half], (far2.at[array, half], near2.at[array, half])
            out.append(
                Reduce(
                    ring,
                    part,
                    *inbox,
                    send.at[array, half, 2 + phase],
                    recv.at[array, half, 2 + phase],
                )
            )
        return out

    def decay_of(line, tile):
        return jnp.exp2(line[0] * rate_ref[:, tile])

    states = rate_ref.shape[0]

    def joined(box, low_first):
        tiles = tiles_of(channels)

        def one(i, carried):
            gap, held_state = carried
            other = ctx - 1 - i if low_first else ctx + 1 + i
            (ends if low_first else backs).wait_one(other)
            totals.wait_one(other)
            made = tuple(
                h
                + jnp.exp2(gap[:, tile] * rate_ref[:, tile]) * box[other, :, tile].astype(f32)
                for tile, h in zip(tiles, held_state)
            )
            return gap + sum_box[other], made

        count = ctx if low_first else ctx_count - 1 - ctx
        zero = tuple(jnp.zeros((states, LANES), f32) for _ in tiles)
        return lax.fori_loop(0, count, one, (jnp.zeros((1, channels), f32), zero))[1]

    sums[...] = jnp.sum(delta_ref[...], axis=0, keepdims=True)
    d_out = dout_ref[...].astype(f32)
    to_slabs(
        COT,
        sum(
            jnp.dot(
                place_ref[k],
                quarters((weight_ref[:, k : k + 1] * d_out).astype(bf16)),
                preferred_element_type=f32,
            )
            for k in (0, 1)
        ),
    )
    barrier_with(("ctx", "exp"))
    totals.start(0, ctx)
    totals.start(ctx + 1, ctx_count)
    moves[COT].start()
    drive[...] = delta_ref[...] * u_ref[...].astype(f32)

    def end_step(t, tile, line, h):
        return decay_of(line, tile) * h + brep_ref[t] * line[1], None

    done = scan_tokens(seg_rows, channels, (delta_ref, drive), end_step, zero_state(rate_ref))
    for tile, h in zip(tiles_of(channels), done):
        end16[:, tile] = h.astype(bf16)
    ends.start(ctx + 1, ctx_count)
    moves[COT].wait()
    take_in(1, COT)

    def out_step(t, tile, line, h):
        new = decay_of(line, tile) * h + brep_ref[t] * line[1]
        return new, jnp.sum(crep_ref[t] * new, axis=0, keepdims=True)

    scan_tokens(seg_rows, channels, (delta_ref, drive), out_step, joined(end_box, True), y)
    gated[...] = (
        (y[...] + skip_ref[...] * u_ref[...].astype(f32)) * silu(z_ref[...].astype(f32))
    ).astype(bf16)
    step = 512
    for n in range(width // step):
        tile = slice(n * step, (n + 1) * step)
        value = (
            jnp.dot(gated[...], wout_ref[:, tile], preferred_element_type=f32)
            .astype(bf16)
            .reshape(z_count, 2, my_rows, step)
        )
        for k in (0, 1):
            mixed[k, :, :, tile] = value[:, k]
    pair = remote(
        mixed.at[1 - core], pair_box, mix_send.at[z], mix_recv.at[z], sibling
    )
    pair.start()
    spread_out(1)
    pair.wait_recv()

    def mix(other, slot):
        return remote(
            mixed.at[core, other],
            mix_box.at[slot],
            mix_send.at[other],
            mix_recv.at[slot],
            {"exp": other * 2 + core},
        )

    def mix_start(d):
        other = (z + d) % z_count
        add_into(mixed.at[core, other], pair_box.at[other])
        mix(other, z).start()

    each(1, z_count, mix_start)
    stream[...] = (
        resid_ref[...].astype(f32) + mixed[core, z].astype(f32) + pair_box[z].astype(f32)
    )

    def mix_take(d):
        other = (z + d) % z_count
        mix(other, other).wait_recv()
        stream[...] += mix_box[other].astype(f32)

    each(1, z_count, mix_take)
    flow = stream[...]
    inverse = lax.rsqrt(jnp.mean(flow * flow, axis=-1, keepdims=True) + 1e-05)
    normed = (flow * inverse * gain_ref[...]).astype(bf16)
    spread = place_ref[0] + place_ref[1]
    to_slabs(ROW, jnp.dot(spread, quarters(normed), preferred_element_type=f32))
    moves[ROW].start()
    for g in far_gathers[1]:
        g.before()
        g.after()
    moves[ROW].wait()
    take_in(0, ROW)
    spread_out(0)

    both = SIDE * rows

    def group(k, carried):
        @pl.when(k == 0)
        def _():
            for g in far_gathers[1]:
                g.across()

        @pl.when(k == 1)
        def _():
            for g in far_gathers[0]:
                g.before()

        @pl.when(k == 2)
        def _():
            for g in far_gathers[0]:
                g.after()

        @pl.when(k == 3)
        def _():
            for g in far_gathers[0]:
                g.across()

        shift = jnp.where(k == 0, 0, jnp.where(k == 1, SIDE - 1, jnp.where(k == 2, 1, 2)))
        places = [(second[h].place + shift) % SIDE for h in (0, 1)]

        def taken(array):
            return jnp.concatenate(
                [held[array, h, places[h]].reshape(both, width) for h in (0, 1)], axis=0
            )

        def put(array, tile, value):
            value = value.astype(bf16)
            for h in (0, 1):
                parts[array, h, places[h], :, :, tile] = value[
                    h * both : (h + 1) * both
                ].reshape(SIDE, rows, -1)

        x = taken(0)
        gate = jnp.dot(x, wg_ref[...], preferred_element_type=f32)
        up = jnp.dot(x, wu_ref[...], preferred_element_type=f32)
        hidden_grad = contract_last(taken(1), wd_ref[...])
        sigma = 1.0 / (1.0 + jnp.exp(-gate))
        active = gate * sigma
        hidden = (active * up).astype(bf16)
        gate_grad = (hidden_grad * up * sigma * (1.0 + gate * (1.0 - sigma))).astype(bf16)
        up_grad = (hidden_grad * active).astype(bf16)
        for n in range(width // step):
            tile = slice(n * step, (n + 1) * step)
            put(
                1,
                tile,
                contract_last(gate_grad, wg_ref[tile, :]) + contract_last(up_grad, wu_ref[tile, :]),
            )

        @pl.when(k == 3)
        def _():
            for r in reduces(1, 0):
                r.start()

        for n in range(width // step):
            tile = slice(n * step, (n + 1) * step)
            put(0, tile, jnp.dot(hidden, wd_ref[:, tile], preferred_element_type=f32))
        return carried

    lax.fori_loop(0, SIDE, group, 0)
    grads, outs = reduces(1, 0), reduces(0, 0)
    grads2, outs2 = reduces(1, 1), reduces(0, 1)
    for r in grads:
        r.middle()
    for half in (0, 1):
        own2[1, half] = grads[half].total()
        grads2[half].start()
    for r in outs:
        r.start()
    for r in grads2:
        r.middle()
    sent = [r.total() for r in grads2]
    give_back(GRAD, lambda tile: jnp.concatenate([v[:, tile] for v in sent], axis=0))
    moves[GRAD].start()
    moves[GRAD].wait()

    def combined(kind, matrix):
        flat = boxes[kind].reshape(exp_count * slab_rows, slab_width)
        return whole(jnp.dot(matrix, flat, preferred_element_type=f32))

    scaled = combined(GRAD, placet_ref[0] + placet_ref[1]) * gain_ref[...]
    flow = stream[...]
    inverse = lax.rsqrt(jnp.mean(flow * flow, axis=-1, keepdims=True) + 1e-05)
    project = jnp.mean(scaled * flow, axis=-1, keepdims=True)
    grad_rows = (
        dout_ref[...].astype(f32) + inverse * (scaled - flow * inverse * inverse * project)
    ).astype(bf16)
    gresid_ref[...] = grad_rows
    segment[exp] = grad_rows

    def seg(target, slot):
        return remote(
            segment.at[exp],
            segment.at[slot],
            seg_send.at[0, target],
            seg_recv.at[0, slot // 2],
            {"exp": target * 2 + core},
        )

    def seg_pair(slot):
        return remote(
            segment.at[slot],
            segment.at[slot],
            seg_send.at[1, slot // 2],
            seg_recv.at[1, slot // 2],
            sibling,
        )

    each(1, z_count, lambda d: seg((z + d) % z_count, exp).start())
    seg_pair(exp).start()
    for r in outs:
        r.middle()

    def seg_take(d):
        other = ((z + d) % z_count) * 2 + core
        seg((z + d) % z_count, other).wait_recv()
        seg_pair(other).start()

    each(1, z_count, seg_take)
    for half in (0, 1):
        own2[0, half] = outs[half].total()
        outs2[half].start()
    each(0, z_count, lambda i: seg_pair(i * 2 + 1 - core).wait_recv())
    grad = drive
    grad[...] = contract_last(
        segment[...].reshape(seg_rows, width), wout_ref[...]
    ) * silu(z_ref[...].astype(f32))

    def back_end_step(t, tile, line, h):
        return decay_of(line, tile) * (h + crep_ref[t] * line[1]), None

    done = scan_tokens(
        seg_rows, channels, (delta_ref, grad), back_end_step, zero_state(rate_ref), backward=True
    )
    for tile, h in zip(tiles_of(channels), done):
        back16[:, tile] = h.astype(bf16)
    backs.start(0, ctx)
    for r in outs2:
        r.middle()
    sent = [r.total() for r in outs2]
    give_back(OUT, lambda tile: jnp.concatenate([v[:, tile] for v in sent], axis=0))
    moves[OUT].start()

    def back_step(t, tile, line, h):
        new = h + crep_ref[t] * line[1]
        return decay_of(line, tile) * new, jnp.sum(brep_ref[t] * new, axis=0, keepdims=True)

    scan_tokens(
        seg_rows,
        channels,
        (delta_ref, grad),
        back_step,
        joined(back_box, False),
        y,
        backward=True,
    )
    gradu_ref[...] = (delta_ref[...] * y[...] + skip_ref[...] * grad[...]).astype(bf16)
    moves[OUT].wait()
    final_ref[...] = (
        stream[...]
        + weight_ref[:, 0:1] * combined(OUT, placet_ref[0])
        + weight_ref[:, 1:2] * combined(OUT, placet_ref[1])
    ).astype(bf16)

    for array in (0, 1):
        for g in near_gathers[array] + far_gathers[array]:
            g.finish()
    for r in grads + outs + grads2 + outs2:
        r.finish()
    for m in moves:
        m.finish()
    pair.wait_send()
    totals.finish(0, ctx)
    totals.finish(ctx + 1, ctx_count)
    ends.finish(ctx + 1, ctx_count)
    backs.finish(0, ctx)
    each(1, z_count, lambda d: mix((z + d) % z_count, z).wait_send())
    each(1, z_count, lambda d: seg((z + d) % z_count, exp).wait_send())
    each(0, z_count, lambda i: seg_pair(i * 2 + core).wait_send())


def layer(args, exp_count, ctx_count):
    delta, rate, resid = args[0], args[5], args[8]
    seg_rows, channels = delta.shape
    states = rate.shape[0]
    my_rows, width = resid.shape
    bf16, f32 = jnp.bfloat16, jnp.float32
    slots = 4 * my_rows // exp_count
    half = exp_count * slots // 2
    vm, dma = pltpu.VMEM, pltpu.SemaphoreType.DMA
    full = vm((2, 2, SIDE, SIDE, half, width), bf16)
    plane = vm((seg_rows, channels), f32)
    slab = vm((4, exp_count, 4 * slots, width // 4), bf16)
    state_box = vm((ctx_count, states, channels), bf16)
    shape = jax.ShapeDtypeStruct
    return pl.pallas_call(
        layer_kernel,
        out_shape=[
            shape((my_rows, width), bf16),
            shape((my_rows, width), bf16),
            shape((seg_rows, channels), bf16),
        ],
        in_specs=[VMEM] * len(args),
        out_specs=[VMEM] * 3,
        scratch_shapes=[
            plane,
            plane,
            vm((seg_rows, channels), bf16),
            vm((states, channels), bf16),
            vm((states, channels), bf16),
            vm((1, channels), f32),
            state_box,
            vm((ctx_count, 1, channels), f32),
            state_box,
            dma((3, ctx_count)),
            dma((3, ctx_count)),
            vm((2, exp_count // 2, my_rows, width), bf16),
            vm((exp_count // 2, my_rows, width), bf16),
            vm((exp_count // 2, my_rows, width), bf16),
            dma((exp_count // 2,)),
            dma((exp_count // 2,)),
            slab,
            slab,
            dma((4, exp_count)),
            dma((4, exp_count)),
            vm((my_rows, width), f32),
            vm((exp_count, my_rows, width), bf16),
            dma((2, exp_count // 2)),
            dma((2, exp_count // 2)),
            full,
            full,
            vm((2, 2, 2, SIDE // 2, half, width), bf16),
            vm((2, 2, 2, SIDE, half, width), bf16),
            vm((2, 2, SIDE, half, width), bf16),
            vm((2, 2, 2, half // 2, width), bf16),
            vm((2, 2, 2, half, width), bf16),
            dma((2, 2, 4, 4)),
            dma((2, 2, 4, 4)),
        ],
        compiler_params=pltpu.CompilerParams(
            vmem_limit_bytes=60 * 1024 * 1024, collective_id=1, has_side_effects=True
        ),
    )(*args)


def local(
    u_in,
    z_gate,
    delta,
    b_in,
    c_in,
    rate,
    skip,
    w_out,
    resid,
    gain,
    expert_ids,
    route_weights,
    w_gate,
    w_up,
    w_down,
    d_out,
):
    seg_rows, channels = u_in.shape
    states = rate.shape[0]
    my_rows, width = resid.shape
    experts_count = lax.axis_size("exp")
    capacity = 4 * my_rows // experts_count
    f32 = jnp.float32
    rate2 = rate * (-math.log2(math.e))
    brep = jnp.broadcast_to(b_in[:, :, None], (seg_rows, states, LANES))
    crep = jnp.broadcast_to(c_in[:, :, None], (seg_rows, states, LANES))
    owners = expert_ids.reshape(-1)
    assign_count = owners.shape[0]
    onehot = (owners[:, None] == jnp.arange(experts_count, dtype=jnp.int32)[None, :]).astype(
        jnp.float32
    )
    assign_index = jnp.arange(assign_count)
    strict = (assign_index[:, None] > assign_index[None, :]).astype(jnp.float32)
    before = jnp.dot(strict, onehot, precision=lax.Precision.HIGHEST)
    slots = jnp.sum(before * onehot, axis=1).astype(jnp.int32)
    target = owners * capacity + slots
    row = jnp.arange(4 * experts_count * capacity, dtype=jnp.int32)[:, None]
    column = jnp.arange(4 * my_rows, dtype=jnp.int32)[None, :]
    slab = 4 * capacity
    code = (row // slab) * capacity + row % capacity
    same = (row % slab) // capacity == column // my_rows
    targets = target.reshape(my_rows, 2)
    place = jnp.stack(
        [same & (code == jnp.tile(targets[:, k], 4)[None, :]) for k in (0, 1)]
    ).astype(jnp.bfloat16)
    return tuple(
        layer(
            (
                delta,
                u_in,
                z_gate,
                brep,
                crep,
                rate2,
                skip[None, :],
                w_out,
                resid,
                gain[None, :],
                route_weights,
                place,
                jnp.swapaxes(place, 1, 2),
                w_gate[0],
                w_up[0],
                w_down[0],
                d_out,
            ),
            experts_count,
            lax.axis_size("ctx"),
        )
    )


def solution(mesh):
    return jax.shard_map(
        local,
        mesh=mesh,
        in_specs=(
            P("ctx", "exp"),
            P("ctx", "exp"),
            P("ctx", "exp"),
            P("ctx", None),
            P("ctx", None),
            P(None, "exp"),
            P("exp"),
            P("exp", None),
            P(("ctx", "exp"), None),
            P(),
            P(("ctx", "exp"), None),
            P(("ctx", "exp"), None),
            P("exp", None, "ctx"),
            P("exp", None, "ctx"),
            P("exp", "ctx", None),
            P(("ctx", "exp"), None),
        ),
        out_specs=(P(("ctx", "exp"), None), P(("ctx", "exp"), None), P("ctx", "exp")),
        check_vma=False,
    )
```

time: 372 us -> 187 us (0.50); the launches traced: 367 us -> 187 us
  waiting for transfers between devices: 108 us -> 0 us
  blocking collectives: 57.2 us -> 0 us
  Pallas kernels: 118 us -> 170 us
  starting transfers between devices: 40.3 us -> 0 us
  between operations: 14.4 us -> 0.67 us
  matrix products: 7.6 us -> 0.14 us
  other arithmetic: 7.09 us -> 2.83 us
    all_gather x3 -> x0, blocking collectives: 57.2 us -> none  [the longest x1 21.7 us: local(): ends = lax.all_gather(state_end.astype(jnp.bfloat16), 'ctx')]
    pallas_call x5 -> x1, Pallas kernels: 118 us -> 170 us  [layer(): pl.pallas_call(layer_kernel, out_shape=[shape((my_rows, width), bf16), sh...]
    reduce_scatter x1 -> x0, waiting for transfers between devices: 45.9 us -> none  [local(): lax.psum_scatter(jnp.dot(gated, w_out, preferred_element_type=jnp.float32...]
    all_to_all x4 -> x0, starting transfers between devices: 40.3 us -> none  [the longest x1 20 us: local(): lax.all_to_all(grad_outgoing, 'exp', split_axis=0, concat_axis=0, tiled=T...]
    all_gather x1 -> x0, waiting for transfers between devices: 33.4 us -> none  [local(): segment_grad = lax.all_gather(grad_resid, 'exp', axis=0, tiled=True)]
    all_to_all x4 -> x0, waiting for transfers between devices: 29 us -> none  [the longest x1 10.9 us: local(): lax.all_to_all(outgoing, 'exp', split_axis=0, concat_axis=0, tiled=True)]
    reshape x11 -> x0, local copies, waits for them, and re-layouts: 9.19 us -> none  [the longest x1 1.76 us: local(): summed = summed.reshape(arrived.shape)]
    dot_general x6 -> x0, matrix products: 7.46 us -> none  [the longest x1 2.12 us: contract_last(): lax.dot_general(left, right, (((1,), (1,)), ((), ())), preferred_element_...]
  transfers between devices with their start and end apart: 6 -> 0, of which waited for: 5 -> 0; matrix products, arithmetic and copies ran while one was open for 3% -> 0% of each run, Pallas kernels for 0% -> 0%
where the time goes in v2:
time: 187 us
  Pallas kernels  170 us (91%)
  local copies, waits for them, and re-layouts  13.4 us (7%)
  other arithmetic  2.83 us (2%)
    pallas_call x1, Pallas kernels, layer(): pl.pallas_call(layer_kernel, out_shape=[shape((my_rows, width), bf16), sh...  170 us
    unnamed x7, local copies, waits for them, and re-layouts  8.36 us

profile of v2, /device:TPU:1, one launch (start us, length us, event | category | flops | bytes accessed | tf_op | source)
XLA Modules:
  0.0 186.8 jit_solution(8332153102457396966)
XLA Ops:
  0.7 1.4 copy.37.weight_ref
  2.0 0.8 copy.35
  2.8 0.1 eq.96
  2.9 0.1 fusion
  3.0 0.1 convert_element_type.13
  3.1 0.1 copy.36
  3.2 0.7 multiply_add_fusion
  3.9 0.1 eq.100
  4.0 0.1 eq.103
  4.1 0.1 compare_and_fusion.1
  4.2 1.4 broadcast_multiply_fusion.rate_ref
  5.5 0.6 fusion.5
  6.2 0.8 copy.38.place_ref
  6.9 0.8 copy.33
  7.8 0.8 copy.34
  8.6 1.9 %broadcast_in_dim.9.crep_ref = f32[256,16,128]{2,1,0:T(8,128)} broadcast(f32[256,16]{1,0:T(8,128)S(1)} %copy.34), dimensions={0,1} | broadcast | bytes 2113536 | tf_op jit(solution)/shard_map/broadcast_in_dim | solution.py:837
  10.5 1.9 %broadcast_in_dim.8.brep_ref = f32[256,16,128]{2,1,0:T(8,128)} broadcast(f32[256,16]{1,0:T(8,128)S(1)} %copy.33), dimensions={0,1} | broadcast | bytes 2113536 | tf_op jit(solution)/shard_map/broadcast_in_dim | solution.py:836
  12.4 169.8 %shard_map.175 = (bf16[16,2048]{1,0:T(8,128)(2,1)}, bf16[16,2048]{1,0:T(8,128)(2,1)}, bf16[256,512]{1,0:T(8,128)(2,1)}) custom-call(f32[256,512]{1,0:T(8,128)} %delta_ref.1, bf16[256,512]{1,0:T(8,128)(2,1)} %u_ref.1, bf16[256,512]{1,0:T(8,128)(2,1)} %z_ref.1, f32[256,16,128]{2,1,0:T(8,128)} %broadcast_in_dim.8.brep_ref, ...), custom_call_target="tpu_custom_call" | custom-call | tf_op jit(solution)/shard_map/pallas_call | solution.py:761
  182.2 1.5 copy.42
  183.7 1.5 copy.43
  185.2 1.7 copy.44
  (6 shorter events, 0.0 us)

commit v3 on v2

--- a/solution.py
+++ b/solution.py
@@ -292,27 +292,96 @@
     return jnp.concatenate([value[q * step : (q + 1) * step] for q in range(4)], axis=1)
 
 
+def as_column(row):
+    count = row.shape[1]
+    line = lax.broadcasted_iota(jnp.int32, (count, count), 0)
+    column = lax.broadcasted_iota(jnp.int32, (count, count), 1)
+    return jnp.sum(jnp.where(line == column, row, 0.0), axis=1, keepdims=True)
+
+
+def make_places(ids_ref, place_ref, placet_ref, experts, slots, tokens):
+    f32, i32 = jnp.float32, jnp.int32
+    iota = lax.broadcasted_iota
+    ids = [as_column(ids_ref[k : k + 1, :].astype(f32)) for k in (0, 1)]
+    names = iota(i32, (tokens, experts), 1).astype(f32)
+    onehot = [jnp.where(names == c, 1.0, 0.0) for c in ids]
+    earlier = iota(i32, (tokens, tokens), 0) > iota(i32, (tokens, tokens), 1)
+    before = jnp.dot(
+        jnp.where(earlier, 1.0, 0.0).astype(jnp.bfloat16),
+        (onehot[0] + onehot[1]).astype(jnp.bfloat16),
+        preferred_element_type=f32,
+    )
+    slab = 4 * slots
+
+    def codes(size, axis):
+        row = iota(i32, size, axis)
+        return ((row // slab) * slots + row % slots).astype(f32), (row % slab) // slots
+
+    wide = 4 * experts * slots
+    for k in (0, 1):
+        target = ids[k] * slots + jnp.sum(before * onehot[k], axis=1, keepdims=True)
+        place = iota(i32, (tokens, 4 * tokens), 1) % tokens
+        own = place == iota(i32, (tokens, 4 * tokens), 0)
+        target_row = jnp.sum(jnp.where(own, target, 0.0), axis=0, keepdims=True)
+        code, quarter = codes((wide, 4 * tokens), 0)
+        same = quarter == iota(i32, (wide, 4 * tokens), 1) // tokens
+        place_ref[k] = jnp.where(
+            jnp.logical_and(same, code == target_row), 1.0, 0.0
+        ).astype(place_ref.dtype)
+        code, quarter = codes((4 * tokens, wide), 1)
+        same = quarter == iota(i32, (4 * tokens, wide), 0) // tokens
+        target_column = jnp.concatenate([target] * 4, axis=0)
+        placet_ref[k] = jnp.where(
+            jnp.logical_and(same, code == target_column), 1.0, 0.0
+        ).astype(placet_ref.dtype)
+
+
+def spread_lanes(source_ref, target_ref):
+    states, count = source_ref.shape
+
+    def some(i, carried):
+        for part in range(count // LANES):
+            lanes = source_ref[:, part * LANES : (part + 1) * LANES]
+            turned = pltpu.roll(lanes, (LANES - i * GROUP) % LANES, 1)
+            for j in range(GROUP):
+                target_ref[part * LANES + i * GROUP + j] = jnp.broadcast_to(
+                    turned[:, j : j + 1], (states, LANES)
+                )
+        return carried
+
+    lax.fori_loop(0, LANES // GROUP, some, 0)
+
+
 def layer_kernel(
     delta_ref,
     u_ref,
     z_ref,
-    brep_ref,
-    crep_ref,
-    rate_ref,
+    b_ref,
+    c_ref,
+    plain_rate_ref,
     skip_ref,
-    wout_ref,
+    wout_hbm,
     resid_ref,
     gain_ref,
+    ids_ref,
     weight_ref,
-    place_ref,
-    placet_ref,
-    wg_ref,
-    wu_ref,
-    wd_ref,
+    wg_hbm,
+    wu_hbm,
+    wd_hbm,
     dout_ref,
     final_ref,
     gresid_ref,
     gradu_ref,
+    brep_ref,
+    crep_ref,
+    rate_ref,
+    wout_ref,
+    wg_ref,
+    wu_ref,
+    wd_ref,
+    weight_sem,
+    place_ref,
+    placet_ref,
     drive,
     y,
     gated,
@@ -326,6 +395,8 @@
     state_recv,
     mixed,
     pair_box,
+    pair_send,
+    pair_recv,
     mix_box,
     mix_send,
     mix_recv,
@@ -337,6 +408,8 @@
     segment,
     seg_send,
     seg_recv,
+    twin_send,
+    twin_recv,
     held,
     parts,
     far,
@@ -465,14 +538,25 @@
         zero = tuple(jnp.zeros((states, LANES), f32) for _ in tiles)
         return lax.fori_loop(0, count, one, (jnp.zeros((1, channels), f32), zero))[1]
 
+    fetches = [
+        pltpu.make_async_copy(source, target, weight_sem.at[i])
+        for i, (source, target) in enumerate(
+            ((wout_hbm, wout_ref), (wd_hbm, wd_ref), (wg_hbm, wg_ref), (wu_hbm, wu_ref))
+        )
+    ]
+    for f in fetches:
+        f.start()
     sums[...] = jnp.sum(delta_ref[...], axis=0, keepdims=True)
+    rate_ref[...] = plain_rate_ref[...] * (-math.log2(math.e))
+    make_places(ids_ref, place_ref, placet_ref, exp_count, slots, my_rows)
+    columns = [as_column(weight_ref[k : k + 1, :]) for k in (0, 1)]
     d_out = dout_ref[...].astype(f32)
     to_slabs(
         COT,
         sum(
             jnp.dot(
                 place_ref[k],
-                quarters((weight_ref[:, k : k + 1] * d_out).astype(bf16)),
+                quarters((columns[k] * d_out).astype(bf16)),
                 preferred_element_type=f32,
             )
             for k in (0, 1)
@@ -482,6 +566,7 @@
     totals.start(0, ctx)
     totals.start(ctx + 1, ctx_count)
     moves[COT].start()
+    spread_lanes(b_ref, brep_ref)
     drive[...] = delta_ref[...] * u_ref[...].astype(f32)
 
     def end_step(t, tile, line, h):
@@ -491,6 +576,7 @@
     for tile, h in zip(tiles_of(channels), done):
         end16[:, tile] = h.astype(bf16)
     ends.start(ctx + 1, ctx_count)
+    spread_lanes(c_ref, crep_ref)
     moves[COT].wait()
     take_in(1, COT)
 
@@ -503,6 +589,7 @@
         (y[...] + skip_ref[...] * u_ref[...].astype(f32)) * silu(z_ref[...].astype(f32))
     ).astype(bf16)
     step = 512
+    fetches[0].wait()
     for n in range(width // step):
         tile = slice(n * step, (n + 1) * step)
         value = (
@@ -512,38 +599,59 @@
         )
         for k in (0, 1):
             mixed[k, :, :, tile] = value[:, k]
-    pair = remote(
-        mixed.at[1 - core], pair_box, mix_send.at[z], mix_recv.at[z], sibling
-    )
+    pair = remote(mixed.at[1 - core], pair_box, pair_send.at[0], pair_recv.at[0], sibling)
     pair.start()
     spread_out(1)
     pair.wait_recv()
 
-    def mix(other, slot):
+    RIGHT, LEFT = 0, 1
+    hops = z_count // 2
+    middle = width // 2
+    beside = [
+        {"exp": ((z + 1) % z_count) * 2 + core},
+        {"exp": ((z + z_count - 1) % z_count) * 2 + core},
+    ]
+
+    def at_distance(way, far_by):
+        return (z + far_by) % z_count if way == RIGHT else (z + z_count - far_by) % z_count
+
+    def side(ref, way, halved):
+        return ref.at[:, pl.ds(way * middle, middle)] if halved else ref
+
+    def mix(way, hop):
         return remote(
-            mixed.at[core, other],
-            mix_box.at[slot],
-            mix_send.at[other],
-            mix_recv.at[slot],
-            {"exp": other * 2 + core},
+            side(mixed.at[core, at_distance(way, hops - hop)], way, hop == 0),
+            side(mix_box.at[way, hop], way, hop == 0),
+            mix_send.at[way, hop],
+            mix_recv.at[way, hop],
+            beside[way],
         )
 
-    def mix_start(d):
+    add_into(mixed.at[core, at_distance(RIGHT, hops)], pair_box.at[at_distance(RIGHT, hops)])
+    for way in (RIGHT, LEFT):
+        mix(way, 0).start()
+
+    def add_pair(d):
         other = (z + d) % z_count
         add_into(mixed.at[core, other], pair_box.at[other])
-        mix(other, z).start()
-
-    each(1, z_count, mix_start)
+
+    each(hops + 1, z_count + hops, add_pair)
+    for hop in range(1, hops):
+        for way in (RIGHT, LEFT):
+            mix(way, hop - 1).wait_recv()
+            add_into(
+                side(mixed.at[core, at_distance(way, hops - hop)], way, hop == 1),
+                side(mix_box.at[way, hop - 1], way, hop == 1),
+            )
+            mix(way, hop).start()
+    for way in (RIGHT, LEFT):
+        mix(way, hops - 1).wait_recv()
     stream[...] = (
-        resid_ref[...].astype(f32) + mixed[core, z].astype(f32) + pair_box[z].astype(f32)
+        resid_ref[...].astype(f32)
+        + mixed[core, z].astype(f32)
+        + mix_box[RIGHT, hops - 1].astype(f32)
+        + mix_box[LEFT, hops - 1].astype(f32)
     )
-
-    def mix_take(d):
-        other = (z + d) % z_count
-        mix(other, other).wait_recv()
-        stream[...] += mix_box[other].astype(f32)
-
-    each(1, z_count, mix_take)
     flow = stream[...]
     inverse = lax.rsqrt(jnp.mean(flow * flow, axis=-1, keepdims=True) + 1e-05)
     normed = (flow * inverse * gain_ref[...]).astype(bf16)
@@ -557,6 +665,8 @@
     take_in(0, ROW)
     spread_out(0)
 
+    for f in fetches[1:]:
+        f.wait()
     both = SIDE * rows
 
     def group(k, carried):
@@ -637,6 +747,8 @@
     sent = [r.total() for r in grads2]
     give_back(GRAD, lambda tile: jnp.concatenate([v[:, tile] for v in sent], axis=0))
     moves[GRAD].start()
+    for r in outs:
+        r.middle()
     moves[GRAD].wait()
 
     def combined(kind, matrix):
@@ -653,43 +765,42 @@
     gresid_ref[...] = grad_rows
     segment[exp] = grad_rows
 
-    def seg(target, slot):
-        return remote(
-            segment.at[exp],
-            segment.at[slot],
-            seg_send.at[0, target],
-            seg_recv.at[0, slot // 2],
-            {"exp": target * 2 + core},
-        )
-
-    def seg_pair(slot):
+    def seg(way, hop, came=False):
+        block = segment.at[at_distance(1 - way, hop + (1 if came else 0)) * 2 + core]
+        block = side(block, way, hop == hops - 1)
+        return remote(block, block, seg_send.at[way, hop], seg_recv.at[way, hop], beside[way])
+
+    def twin(slot):
         return remote(
             segment.at[slot],
             segment.at[slot],
-            seg_send.at[1, slot // 2],
-            seg_recv.at[1, slot // 2],
+            twin_send.at[slot // 2],
+            twin_recv.at[slot // 2],
             sibling,
         )
 
-    each(1, z_count, lambda d: seg((z + d) % z_count, exp).start())
-    seg_pair(exp).start()
-    for r in outs:
-        r.middle()
-
-    def seg_take(d):
-        other = ((z + d) % z_count) * 2 + core
-        seg((z + d) % z_count, other).wait_recv()
-        seg_pair(other).start()
-
-    each(1, z_count, seg_take)
+    for way in (RIGHT, LEFT):
+        seg(way, 0).start()
+    twin(exp).start()
+    for hop in range(1, hops):
+        for way in (RIGHT, LEFT):
+            seg(way, hop - 1, True).wait_recv()
+            seg(way, hop).start()
+            twin(at_distance(1 - way, hop) * 2 + core).start()
+    for way in (RIGHT, LEFT):
+        seg(way, hops - 1, True).wait_recv()
+    twin(at_distance(RIGHT, hops) * 2 + core).start()
     for half in (0, 1):
         own2[0, half] = outs[half].total()
         outs2[half].start()
-    each(0, z_count, lambda i: seg_pair(i * 2 + 1 - core).wait_recv())
+    each(0, z_count, lambda i: twin(i * 2 + 1 - core).wait_recv())
     grad = drive
     grad[...] = contract_last(
         segment[...].reshape(seg_rows, width), wout_ref[...]
     ) * silu(z_ref[...].astype(f32))
+
+    for r in outs2:
+        r.middle()
 
     def back_end_step(t, tile, line, h):
         return decay_of(line, tile) * (h + crep_ref[t] * line[1]), None
@@ -700,8 +811,6 @@
     for tile, h in zip(tiles_of(channels), done):
         back16[:, tile] = h.astype(bf16)
     backs.start(0, ctx)
-    for r in outs2:
-        r.middle()
     sent = [r.total() for r in outs2]
     give_back(OUT, lambda tile: jnp.concatenate([v[:, tile] for v in sent], axis=0))
     moves[OUT].start()
@@ -723,8 +832,8 @@
     moves[OUT].wait()
     final_ref[...] = (
         stream[...]
-        + weight_ref[:, 0:1] * combined(OUT, placet_ref[0])
-        + weight_ref[:, 1:2] * combined(OUT, placet_ref[1])
+        + columns[0] * combined(OUT, placet_ref[0])
+        + columns[1] * combined(OUT, placet_ref[1])
     ).astype(bf16)
 
     for array in (0, 1):
@@ -739,9 +848,26 @@
     totals.finish(ctx + 1, ctx_count)
     ends.finish(ctx + 1, ctx_count)
     backs.finish(0, ctx)
-    each(1, z_count, lambda d: mix((z + d) % z_count, z).wait_send())
-    each(1, z_count, lambda d: seg((z + d) % z_count, exp).wait_send())
-    each(0, z_count, lambda i: seg_pair(i * 2 + core).wait_send())
+    for way in (RIGHT, LEFT):
+        for hop in range(hops):
+            mix(way, hop).wait_send()
+            seg(way, hop).wait_send()
+    each(0, z_count, lambda i: twin(i * 2 + core).wait_send())
+
+
+def settle_kernel(*refs):
+    half = len(refs) // 2
+    for source, target in zip(refs[:half], refs[half:]):
+        target[...] = source[...]
+
+
+def settle(values):
+    return pl.pallas_call(
+        settle_kernel,
+        out_shape=[jax.ShapeDtypeStruct(v.shape, v.dtype) for v in values],
+        in_specs=[VMEM] * len(values),
+        out_specs=[VMEM] * len(values),
+    )(*values)
 
 
 def layer(args, exp_count, ctx_count):
@@ -765,9 +891,19 @@
             shape((my_rows, width), bf16),
             shape((seg_rows, channels), bf16),
         ],
-        in_specs=[VMEM] * len(args),
+        in_specs=[
+            pl.BlockSpec(memory_space=pl.ANY) if i in (7, 12, 13, 14) else VMEM
+            for i in range(len(args))
+        ],
         out_specs=[VMEM] * 3,
         scratch_shapes=[
+            vm((seg_rows, states, LANES), f32),
+            vm((seg_rows, states, LANES), f32),
+            vm((states, channels), f32),
+            *[vm(args[i].shape, bf16) for i in (7, 12, 13, 14)],
+            dma((4,)),
+            vm((2, 4 * exp_count * slots, 4 * my_rows), bf16),
+            vm((2, 4 * my_rows, 4 * exp_count * slots), bf16),
             plane,
             plane,
             vm((seg_rows, channels), bf16),
@@ -781,17 +917,21 @@
             dma((3, ctx_count)),
             vm((2, exp_count // 2, my_rows, width), bf16),
             vm((exp_count // 2, my_rows, width), bf16),
-            vm((exp_count // 2, my_rows, width), bf16),
-            dma((exp_count // 2,)),
-            dma((exp_count // 2,)),
+            dma((1,)),
+            dma((1,)),
+            vm((2, exp_count // 4, my_rows, width), bf16),
+            dma((2, exp_count // 4)),
+            dma((2, exp_count // 4)),
             slab,
             slab,
             dma((4, exp_count)),
             dma((4, exp_count)),
             vm((my_rows, width), f32),
             vm((exp_count, my_rows, width), bf16),
-            dma((2, exp_count // 2)),
-            dma((2, exp_count // 2)),
+            dma((2, exp_count // 4)),
+            dma((2, exp_count // 4)),
+            dma((exp_count // 2,)),
+            dma((exp_count // 2,)),
             full,
             full,
             vm((2, 2, 2, SIDE // 2, half, width), bf16),
@@ -826,57 +966,30 @@
     w_down,
     d_out,
 ):
-    seg_rows, channels = u_in.shape
-    states = rate.shape[0]
-    my_rows, width = resid.shape
-    experts_count = lax.axis_size("exp")
-    capacity = 4 * my_rows // experts_count
-    f32 = jnp.float32
-    rate2 = rate * (-math.log2(math.e))
-    brep = jnp.broadcast_to(b_in[:, :, None], (seg_rows, states, LANES))
-    crep = jnp.broadcast_to(c_in[:, :, None], (seg_rows, states, LANES))
-    owners = expert_ids.reshape(-1)
-    assign_count = owners.shape[0]
-    onehot = (owners[:, None] == jnp.arange(experts_count, dtype=jnp.int32)[None, :]).astype(
-        jnp.float32
-    )
-    assign_index = jnp.arange(assign_count)
-    strict = (assign_index[:, None] > assign_index[None, :]).astype(jnp.float32)
-    before = jnp.dot(strict, onehot, precision=lax.Precision.HIGHEST)
-    slots = jnp.sum(before * onehot, axis=1).astype(jnp.int32)
-    target = owners * capacity + slots
-    row = jnp.arange(4 * experts_count * capacity, dtype=jnp.int32)[:, None]
-    column = jnp.arange(4 * my_rows, dtype=jnp.int32)[None, :]
-    slab = 4 * capacity
-    code = (row // slab) * capacity + row % capacity
-    same = (row % slab) // capacity == column // my_rows
-    targets = target.reshape(my_rows, 2)
-    place = jnp.stack(
-        [same & (code == jnp.tile(targets[:, k], 4)[None, :]) for k in (0, 1)]
-    ).astype(jnp.bfloat16)
     return tuple(
-        layer(
-            (
-                delta,
-                u_in,
-                z_gate,
-                brep,
-                crep,
-                rate2,
-                skip[None, :],
-                w_out,
-                resid,
-                gain[None, :],
-                route_weights,
-                place,
-                jnp.swapaxes(place, 1, 2),
-                w_gate[0],
-                w_up[0],
-                w_down[0],
-                d_out,
-            ),
-            experts_count,
-            lax.axis_size("ctx"),
+        settle(
+            layer(
+                (
+                    delta,
+                    u_in,
+                    z_gate,
+                    b_in.T,
+                    c_in.T,
+                    rate,
+                    skip[None, :],
+                    w_out,
+                    resid,
+                    gain[None, :],
+                    expert_ids.T,
+                    route_weights.T,
+                    w_gate[0],
+                    w_up[0],
+                    w_down[0],
+                    d_out,
+                ),
+                lax.axis_size("exp"),
+                lax.axis_size("ctx"),
+            )
         )
     )
 

time: 187 us -> 168 us (0.90)
  local copies, waits for them, and re-layouts: 13.4 us -> 0 us
  Pallas kernels: 170 us -> 167 us
  other arithmetic: 2.83 us -> 0 us
    unnamed x7 -> x0, local copies, waits for them, and re-layouts: 8.36 us -> none
    pallas_call x1, Pallas kernels: 170 us -> 165 us  [layer(): pl.pallas_call(layer_kernel, out_shape=[shape((my_rows, width), bf16), sh...]
    broadcast_in_dim x2 -> x0, local copies, waits for them, and re-layouts: 3.85 us -> none  [the longest x1 1.94 us: local(): brep = jnp.broadcast_to(b_in[:, :, None], (seg_rows, states, LANES))]
where the time goes in v3:
time: 168 us
  Pallas kernels  167 us (99%)
    pallas_call x1, Pallas kernels, layer(): pl.pallas_call(layer_kernel, out_shape=[shape((my_rows, width), bf16), sh...  165 us

profile of v3, /device:TPU:1, one launch (start us, length us, event | category | flops | bytes accessed | tf_op | source)
XLA Modules:
  0.0 167.7 jit_solution(13073938429823961102)
XLA Ops:
  0.6 165.3 %shard_map.175 = (bf16[16,2048]{1,0:T(8,128)(2,1)}, bf16[16,2048]{1,0:T(8,128)(2,1)}, bf16[256,512]{1,0:T(8,128)(2,1)}) custom-call(f32[256,512]{1,0:T(8,128)} %delta_ref.1, bf16[256,512]{1,0:T(8,128)(2,1)} %u_ref.1, bf16[256,512]{1,0:T(8,128)(2,1)} %z_ref.1, f32[16,256]{1,0:T(8,128)} %bitcast.12, f32[16,256]{1,0:T(8,128)} %bitcast.13, ...), custom_call_target="tpu_custom_call" | custom-call | tf_op jit(solution)/shard_map/pallas_call | solution.py:887
  165.9 1.8 %shard_map.176 = (bf16[16,2048]{1,0:T(8,128)(2,1)}, bf16[16,2048]{1,0:T(8,128)(2,1)}, bf16[256,512]{1,0:T(8,128)(2,1)}) custom-call(bf16[16,2048]{1,0:T(8,128)(2,1)} %get-tuple-element.6.refs_0_, bf16[16,2048]{1,0:T(8,128)(2,1)} %get-tuple-element.7.refs_1_, bf16[256,512]{1,0:T(8,128)(2,1)} %get-tuple-element.8.refs_2_), custom_call_target="tpu_custom_call" | custom-call | tf_op jit(solution)/shard_map/pallas_call | solution.py:865

commit v4 on v3

--- a/solution.py
+++ b/solution.py
@@ -59,9 +59,6 @@
 
 
 SIDE = 4
-TO_RIGHT, TO_LEFT, ON_RIGHT, ON_LEFT = 0, 1, 2, 3
-
-
 class Ring:
     def __init__(self, along_x):
         c = lax.axis_index("ctx")
@@ -79,46 +76,51 @@
 
 
 class Gather:
-    def __init__(self, ring, block, send, recv):
-        self.ring, self.block, self.send, self.recv = ring, block, send, recv
-
-    def copy(self, ref, way):
-        target = self.ring.right if way in (TO_RIGHT, ON_RIGHT) else self.ring.left
+    def __init__(self, ring, block, pieces, send, recv):
+        self.ring, self.block, self.pieces, self.send, self.recv = ring, block, pieces, send, recv
+
+    def copy(self, ref, rightward, sem):
         return pltpu.make_async_remote_copy(
             src_ref=ref,
             dst_ref=ref,
-            send_sem=self.send.at[way],
-            recv_sem=self.recv.at[way],
-            device_id=target,
+            send_sem=self.send.at[sem],
+            recv_sem=self.recv.at[sem],
+            device_id=self.ring.right if rightward else self.ring.left,
             device_id_type=pl.DeviceIdType.MESH,
         )
 
-    def start(self):
-        own = self.block(self.ring.place)
-        self.copy(own, TO_RIGHT).start()
-        self.copy(own, TO_LEFT).start()
+    def piece(self, place, rightward, i):
+        ref = self.block(place)
+        ref = ref if self.pieces == 1 else ref.at[i]
+        return self.copy(ref, rightward, 2 + i if rightward else 2 + self.pieces + i)
+
+    def on(self, place, rightward):
+        return self.copy(halves(self.block(place))[0 if rightward else 1], rightward, 0 if rightward else 1)
+
+    def start(self, i=0):
+        for rightward in (True, False):
+            self.piece(self.ring.place, rightward, i).start()
 
     def before(self):
-        came = self.block(self.ring.before)
-        self.copy(came, TO_RIGHT).wait_recv()
-        self.copy(halves(came)[0], ON_RIGHT).start()
+        for i in range(self.pieces):
+            self.piece(self.ring.before, True, i).wait_recv()
+        self.on(self.ring.before, True).start()
 
     def after(self):
-        came = self.block(self.ring.after)
-        self.copy(came, TO_LEFT).wait_recv()
-        self.copy(halves(came)[1], ON_LEFT).start()
+        for i in range(self.pieces):
+            self.piece(self.ring.after, False, i).wait_recv()
+        self.on(self.ring.after, False).start()
 
     def across(self):
-        first, second = halves(self.block(self.ring.across))
-        self.copy(first, ON_RIGHT).wait_recv()
-        self.copy(second, ON_LEFT).wait_recv()
+        for rightward in (True, False):
+            self.on(self.ring.across, rightward).wait_recv()
 
     def finish(self):
-        own = self.block(self.ring.place)
-        self.copy(own, TO_RIGHT).wait_send()
-        self.copy(own, TO_LEFT).wait_send()
-        self.copy(halves(self.block(self.ring.before))[0], ON_RIGHT).wait_send()
-        self.copy(halves(self.block(self.ring.after))[1], ON_LEFT).wait_send()
+        for rightward in (True, False):
+            for i in range(self.pieces):
+                self.piece(self.ring.place, rightward, i).wait_send()
+        self.on(self.ring.before, True).wait_send()
+        self.on(self.ring.after, False).wait_send()
 
 
 def add_into(total, term):
@@ -127,6 +129,9 @@
     )
 
 
+FAR_RIGHT, FAR_LEFT, ON_RIGHT, ON_LEFT, DIRECT_RIGHT, DIRECT_LEFT = range(6)
+
+
 class Reduce:
     def __init__(self, ring, part, far, near, send, recv):
         self.ring, self.part, self.far, self.near = ring, part, far, near
@@ -134,42 +139,43 @@
 
     def copy(self, way):
         ring = self.ring
-        source = {
-            TO_RIGHT: lambda: halves(self.part(ring.across))[0],
-            TO_LEFT: lambda: halves(self.part(ring.across))[1],
-            ON_RIGHT: lambda: self.part(ring.after),
-            ON_LEFT: lambda: self.part(ring.before),
+        source, target = {
+            FAR_RIGHT: lambda: (halves(self.part(ring.across))[0], self.far.at[0]),
+            FAR_LEFT: lambda: (halves(self.part(ring.across))[1], self.far.at[1]),
+            ON_RIGHT: lambda: (halves(self.part(ring.after))[0], halves(self.near.at[0])[0]),
+            ON_LEFT: lambda: (halves(self.part(ring.before))[1], halves(self.near.at[1])[1]),
+            DIRECT_RIGHT: lambda: (halves(self.part(ring.after))[1], halves(self.near.at[0])[1]),
+            DIRECT_LEFT: lambda: (halves(self.part(ring.before))[0], halves(self.near.at[1])[0]),
         }[way]()
-        target = {
-            TO_RIGHT: self.far.at[0],
-            TO_LEFT: self.far.at[1],
-            ON_RIGHT: self.near.at[0],
-            ON_LEFT: self.near.at[1],
-        }[way]
+        rightward = way in (FAR_RIGHT, ON_RIGHT, DIRECT_RIGHT)
         return pltpu.make_async_remote_copy(
             src_ref=source,
             dst_ref=target,
             send_sem=self.send.at[way],
             recv_sem=self.recv.at[way],
-            device_id=ring.right if way in (TO_RIGHT, ON_RIGHT) else ring.left,
+            device_id=ring.right if rightward else ring.left,
             device_id_type=pl.DeviceIdType.MESH,
         )
 
     def start(self):
-        self.copy(TO_RIGHT).start()
-        self.copy(TO_LEFT).start()
+        self.copy(FAR_RIGHT).start()
+        self.copy(FAR_LEFT).start()
+
+    def direct(self):
+        self.copy(DIRECT_RIGHT).start()
+        self.copy(DIRECT_LEFT).start()
 
     def middle(self):
-        self.copy(TO_RIGHT).wait_recv()
+        self.copy(FAR_RIGHT).wait_recv()
         add_into(halves(self.part(self.ring.after))[0], self.far.at[0])
         self.copy(ON_RIGHT).start()
-        self.copy(TO_LEFT).wait_recv()
+        self.copy(FAR_LEFT).wait_recv()
         add_into(halves(self.part(self.ring.before))[1], self.far.at[1])
         self.copy(ON_LEFT).start()
 
     def total(self):
-        self.copy(ON_RIGHT).wait_recv()
-        self.copy(ON_LEFT).wait_recv()
+        for way in (ON_RIGHT, ON_LEFT, DIRECT_RIGHT, DIRECT_LEFT):
+            self.copy(way).wait_recv()
         f32 = jnp.float32
         own = self.part(self.ring.place)
         return (
@@ -177,7 +183,7 @@
         ).astype(own.dtype)
 
     def finish(self):
-        for way in range(4):
+        for way in range(6):
             self.copy(way).wait_send()
 
 
@@ -467,11 +473,11 @@
     def gather(array, half, phase):
         if phase == 0:
             block = lambda i: held.at[array, half, second[half].place, i]
-            ring = first[half]
+            ring, pieces = first[half], 1
         else:
             block = lambda i: held.at[array, half, i]
-            ring = second[half]
-        return Gather(ring, block, send.at[array, half, phase], recv.at[array, half, phase])
+            ring, pieces = second[half], SIDE
+        return Gather(ring, block, pieces, send.at[array, half, phase], recv.at[array, half, phase])
 
     near_gathers = [[gather(a, h, 0) for h in (0, 1)] for a in (0, 1)]
     far_gathers = [[gather(a, h, 1) for h in (0, 1)] for a in (0, 1)]
@@ -485,14 +491,20 @@
                 ]
         for g in near_gathers[array]:
             g.start()
+        for half in (0, 1):
+            far_gathers[array][half].start(first[half].place)
 
     def spread_out(array):
-        for g in near_gathers[array]:
+        pairs = list(zip(near_gathers[array], far_gathers[array]))
+        for g, h in pairs:
             g.before()
             g.after()
-        for g, h in zip(near_gathers[array], far_gathers[array]):
+        for g, h in pairs:
+            h.start(g.ring.before)
+            h.start(g.ring.after)
+        for g, h in pairs:
             g.across()
-            h.start()
+            h.start(g.ring.across)
 
     def reduces(array, phase):
         out = []
@@ -679,16 +691,14 @@
         def _():
             for g in far_gathers[0]:
                 g.before()
-
-        @pl.when(k == 2)
-        def _():
-            for g in far_gathers[0]:
                 g.after()
 
         @pl.when(k == 3)
         def _():
             for g in far_gathers[0]:
                 g.across()
+            for r in reduces(1, 0):
+                r.direct()
 
         shift = jnp.where(k == 0, 0, jnp.where(k == 1, SIDE - 1, jnp.where(k == 2, 1, 2)))
         places = [(second[h].place + shift) % SIDE for h in (0, 1)]
@@ -740,10 +750,12 @@
     for half in (0, 1):
         own2[1, half] = grads[half].total()
         grads2[half].start()
+        grads2[half].direct()
+    for r in grads2:
+        r.middle()
     for r in outs:
         r.start()
-    for r in grads2:
-        r.middle()
+        r.direct()
     sent = [r.total() for r in grads2]
     give_back(GRAD, lambda tile: jnp.concatenate([v[:, tile] for v in sent], axis=0))
     moves[GRAD].start()
@@ -793,6 +805,7 @@
     for half in (0, 1):
         own2[0, half] = outs[half].total()
         outs2[half].start()
+        outs2[half].direct()
     each(0, z_count, lambda i: twin(i * 2 + 1 - core).wait_recv())
     grad = drive
     grad[...] = contract_last(
@@ -939,8 +952,8 @@
             vm((2, 2, SIDE, half, width), bf16),
             vm((2, 2, 2, half // 2, width), bf16),
             vm((2, 2, 2, half, width), bf16),
-            dma((2, 2, 4, 4)),
-            dma((2, 2, 4, 4)),
+            dma((2, 2, 4, 2 + 2 * SIDE)),
+            dma((2, 2, 4, 2 + 2 * SIDE)),
         ],
         compiler_params=pltpu.CompilerParams(
             vmem_limit_bytes=60 * 1024 * 1024, collective_id=1, has_side_effects=True

time: 168 us -> 160 us (0.952)
  Pallas kernels: 167 us -> 159 us
    pallas_call x1, Pallas kernels: 165 us -> 158 us  [layer(): pl.pallas_call(layer_kernel, out_shape=[shape((my_rows, width), bf16), sh...]
where the time goes in v4:
time: 160 us
  Pallas kernels  159 us (99%)
    pallas_call x1, Pallas kernels, layer(): pl.pallas_call(layer_kernel, out_shape=[shape((my_rows, width), bf16), sh...  158 us

profile of v4, /device:TPU:1, one launch (start us, length us, event | category | flops | bytes accessed | tf_op | source)
XLA Modules:
  0.0 160.1 jit_solution(14161565458479052588)
XLA Ops:
  0.6 157.6 %shard_map.175 = (bf16[16,2048]{1,0:T(8,128)(2,1)}, bf16[16,2048]{1,0:T(8,128)(2,1)}, bf16[256,512]{1,0:T(8,128)(2,1)}) custom-call(f32[256,512]{1,0:T(8,128)} %delta_ref.1, bf16[256,512]{1,0:T(8,128)(2,1)} %u_ref.1, bf16[256,512]{1,0:T(8,128)(2,1)} %z_ref.1, f32[16,256]{1,0:T(8,128)} %bitcast.12, f32[16,256]{1,0:T(8,128)} %bitcast.13, ...), custom_call_target="tpu_custom_call" | custom-call | tf_op jit(solution)/shard_map/pallas_call | solution.py:900
  158.3 1.8 %shard_map.176 = (bf16[16,2048]{1,0:T(8,128)(2,1)}, bf16[16,2048]{1,0:T(8,128)(2,1)}, bf16[256,512]{1,0:T(8,128)(2,1)}) custom-call(bf16[16,2048]{1,0:T(8,128)(2,1)} %get-tuple-element.6.refs_0_, bf16[16,2048]{1,0:T(8,128)(2,1)} %get-tuple-element.7.refs_1_, bf16[256,512]{1,0:T(8,128)(2,1)} %get-tuple-element.8.refs_2_), custom_call_target="tpu_custom_call" | custom-call | tf_op jit(solution)/shard_map/pallas_call | solution.py:878

commit v5 on v4

--- a/solution.py
+++ b/solution.py
@@ -187,7 +187,7 @@
             self.copy(way).wait_send()
 
 
-def barrier_with(axes):
+def greet(axes):
     barrier = pltpu.get_barrier_semaphore()
     total = 0
     for axis in axes:
@@ -205,7 +205,7 @@
 
         lax.fori_loop(1, count, signal, 0)
         total += count - 1
-    pl.semaphore_wait(barrier, total)
+    return lambda: pl.semaphore_wait(barrier, total)
 
 
 def remote(source, target, send, recv, device):
@@ -556,6 +556,7 @@
             ((wout_hbm, wout_ref), (wd_hbm, wd_ref), (wg_hbm, wg_ref), (wu_hbm, wu_ref))
         )
     ]
+    arrived = greet(("ctx", "exp"))
     for f in fetches:
         f.start()
     sums[...] = jnp.sum(delta_ref[...], axis=0, keepdims=True)
@@ -574,12 +575,12 @@
             for k in (0, 1)
         ),
     )
-    barrier_with(("ctx", "exp"))
+    spread_lanes(b_ref, brep_ref)
+    drive[...] = delta_ref[...] * u_ref[...].astype(f32)
+    arrived()
     totals.start(0, ctx)
     totals.start(ctx + 1, ctx_count)
     moves[COT].start()
-    spread_lanes(b_ref, brep_ref)
-    drive[...] = delta_ref[...] * u_ref[...].astype(f32)
 
     def end_step(t, tile, line, h):
         return decay_of(line, tile) * h + brep_ref[t] * line[1], None
@@ -611,11 +612,6 @@
         )
         for k in (0, 1):
             mixed[k, :, :, tile] = value[:, k]
-    pair = remote(mixed.at[1 - core], pair_box, pair_send.at[0], pair_recv.at[0], sibling)
-    pair.start()
-    spread_out(1)
-    pair.wait_recv()
-
     RIGHT, LEFT = 0, 1
     hops = z_count // 2
     middle = width // 2
@@ -627,37 +623,59 @@
     def at_distance(way, far_by):
         return (z + far_by) % z_count if way == RIGHT else (z + z_count - far_by) % z_count
 
-    def side(ref, way, halved):
-        return ref.at[:, pl.ds(way * middle, middle)] if halved else ref
-
-    def mix(way, hop):
+    def side(ref, lane):
+        return ref.at[:, pl.ds(lane * middle, middle)]
+
+    def pair(j):
         return remote(
-            side(mixed.at[core, at_distance(way, hops - hop)], way, hop == 0),
-            side(mix_box.at[way, hop], way, hop == 0),
-            mix_send.at[way, hop],
-            mix_recv.at[way, hop],
+            mixed.at[1 - core, j], pair_box.at[j], pair_send.at[j], pair_recv.at[j], sibling
+        )
+
+    order = [(RIGHT, hops)] + [(w, d) for d in range(hops - 1, 0, -1) for w in (RIGHT, LEFT)]
+    order = [at_distance(w, d) for w, d in order] + [z]
+    for j in order:
+        pair(j).start()
+
+    def paired(j):
+        pair(j).wait_recv()
+        add_into(mixed.at[core, j], pair_box.at[j])
+
+    def mix(way, hop, lane):
+        return remote(
+            side(mixed.at[core, at_distance(way, hops - hop)], lane),
+            side(mix_box.at[way, hop], lane),
+            mix_send.at[way, hop, lane],
+            mix_recv.at[way, hop, lane],
             beside[way],
         )
 
-    add_into(mixed.at[core, at_distance(RIGHT, hops)], pair_box.at[at_distance(RIGHT, hops)])
+    def mix_on(way, hop, lane):
+        mix(way, hop - 1, lane).wait_recv()
+        add_into(
+            side(mixed.at[core, at_distance(way, hops - hop)], lane),
+            side(mix_box.at[way, hop - 1], lane),
+        )
+        mix(way, hop, lane).start()
+
+    paired(order[0])
     for way in (RIGHT, LEFT):
-        mix(way, 0).start()
-
-    def add_pair(d):
-        other = (z + d) % z_count
-        add_into(mixed.at[core, other], pair_box.at[other])
-
-    each(hops + 1, z_count + hops, add_pair)
+        mix(way, 0, way).start()
+    for way in (RIGHT, LEFT):
+        paired(order[1 + way])
+        mix(way, 1, 1 - way).start()
+    for j in order[3:]:
+        paired(j)
     for hop in range(1, hops):
         for way in (RIGHT, LEFT):
-            mix(way, hop - 1).wait_recv()
-            add_into(
-                side(mixed.at[core, at_distance(way, hops - hop)], way, hop == 1),
-                side(mix_box.at[way, hop - 1], way, hop == 1),
-            )
-            mix(way, hop).start()
+            mix_on(way, hop, way)
+        if hop < hops - 1:
+            for way in (RIGHT, LEFT):
+                mix_on(way, hop + 1, 1 - way)
+        if hop == 1:
+            spread_out(1)
     for way in (RIGHT, LEFT):
-        mix(way, hops - 1).wait_recv()
+        for lane in (0, 1):
+            mix(way, hops - 1, lane).wait_recv()
     stream[...] = (
         resid_ref[...].astype(f32)
         + mixed[core, z].astype(f32)
@@ -777,10 +795,12 @@
     gresid_ref[...] = grad_rows
     segment[exp] = grad_rows
 
-    def seg(way, hop, came=False):
+    def seg(way, hop, lane, came=False):
         block = segment.at[at_distance(1 - way, hop + (1 if came else 0)) * 2 + core]
-        block = side(block, way, hop == hops - 1)
-        return remote(block, block, seg_send.at[way, hop], seg_recv.at[way, hop], beside[way])
+        block = side(block, lane)
+        return remote(
+            block, block, seg_send.at[way, hop, lane], seg_recv.at[way, hop, lane], beside[way]
+        )
 
     def twin(slot):
         return remote(
@@ -791,21 +811,26 @@
             sibling,
         )
 
-    for way in (RIGHT, LEFT):
-        seg(way, 0).start()
+    for lane in (0, 1):
+        for way in (RIGHT, LEFT):
+            seg(way, 0, lane if way == LEFT else 1 - lane).start()
     twin(exp).start()
     for hop in range(1, hops):
+        for lane in (0, 1):
+            for way in (RIGHT, LEFT):
+                now = lane if way == LEFT else 1 - lane
+                seg(way, hop - 1, now, True).wait_recv()
+                if hop < hops - 1 or now == way:
+                    seg(way, hop, now).start()
         for way in (RIGHT, LEFT):
-            seg(way, hop - 1, True).wait_recv()
-            seg(way, hop).start()
             twin(at_distance(1 - way, hop) * 2 + core).start()
-    for way in (RIGHT, LEFT):
-        seg(way, hops - 1, True).wait_recv()
-    twin(at_distance(RIGHT, hops) * 2 + core).start()
     for half in (0, 1):
         own2[0, half] = outs[half].total()
         outs2[half].start()
         outs2[half].direct()
+    for way in (RIGHT, LEFT):
+        seg(way, hops - 1, way, True).wait_recv()
+    twin(at_distance(RIGHT, hops) * 2 + core).start()
     each(0, z_count, lambda i: twin(i * 2 + 1 - core).wait_recv())
     grad = drive
     grad[...] = contract_last(
@@ -856,15 +881,18 @@
         r.finish()
     for m in moves:
         m.finish()
-    pair.wait_send()
+    each(0, z_count, lambda j: pair(j).wait_send())
     totals.finish(0, ctx)
     totals.finish(ctx + 1, ctx_count)
     ends.finish(ctx + 1, ctx_count)
     backs.finish(0, ctx)
     for way in (RIGHT, LEFT):
         for hop in range(hops):
-            mix(way, hop).wait_send()
-            seg(way, hop).wait_send()
+            for lane in (0, 1):
+                if hop > 0 or lane == way:
+                    mix(way, hop, lane).wait_send()
+                if hop < hops - 1 or lane == way:
+                    seg(way, hop, lane).wait_send()
     each(0, z_count, lambda i: twin(i * 2 + core).wait_send())
 
 
@@ -930,19 +958,19 @@
             dma((3, ctx_count)),
             vm((2, exp_count // 2, my_rows, width), bf16),
             vm((exp_count // 2, my_rows, width), bf16),
-            dma((1,)),
-            dma((1,)),
+            dma((exp_count // 2,)),
+            dma((exp_count // 2,)),
             vm((2, exp_count // 4, my_rows, width), bf16),
-            dma((2, exp_count // 4)),
-            dma((2, exp_count // 4)),
+            dma((2, exp_count // 4, 2)),
+            dma((2, exp_count // 4, 2)),
             slab,
             slab,
             dma((4, exp_count)),
             dma((4, exp_count)),
             vm((my_rows, width), f32),
             vm((exp_count, my_rows, width), bf16),
-            dma((2, exp_count // 4)),
-            dma((2, exp_count // 4)),
+            dma((2, exp_count // 4, 2)),
+            dma((2, exp_count // 4, 2)),
             dma((exp_count // 2,)),
             dma((exp_count // 2,)),
             full,

time: 160 us -> 152 us (0.950)
  Pallas kernels: 159 us -> 150 us
    pallas_call x1, Pallas kernels: 158 us -> 149 us  [layer(): pl.pallas_call(layer_kernel, out_shape=[shape((my_rows, width), bf16), sh...]
where the time goes in v5:
time: 152 us; the launch traced here: 151 us
  Pallas kernels  150 us (99%)
    pallas_call x1, Pallas kernels, layer(): pl.pallas_call(layer_kernel, out_shape=[shape((my_rows, width), bf16), sh...  149 us

profile of v5, /device:TPU:1, one launch (start us, length us, event | category | flops | bytes accessed | tf_op | source)
XLA Modules:
  0.0 151.0 jit_solution(1971542829014050561)
XLA Ops:
  0.6 148.6 %shard_map.175 = (bf16[16,2048]{1,0:T(8,128)(2,1)}, bf16[16,2048]{1,0:T(8,128)(2,1)}, bf16[256,512]{1,0:T(8,128)(2,1)}) custom-call(f32[256,512]{1,0:T(8,128)} %delta_ref.1, bf16[256,512]{1,0:T(8,128)(2,1)} %u_ref.1, bf16[256,512]{1,0:T(8,128)(2,1)} %z_ref.1, f32[16,256]{1,0:T(8,128)} %bitcast.12, f32[16,256]{1,0:T(8,128)} %bitcast.13, ...), custom_call_target="tpu_custom_call" | custom-call | tf_op jit(solution)/shard_map/pallas_call | solution.py:928
  149.3 1.8 %shard_map.176 = (bf16[16,2048]{1,0:T(8,128)(2,1)}, bf16[16,2048]{1,0:T(8,128)(2,1)}, bf16[256,512]{1,0:T(8,128)(2,1)}) custom-call(bf16[16,2048]{1,0:T(8,128)(2,1)} %get-tuple-element.6.refs_0_, bf16[16,2048]{1,0:T(8,128)(2,1)} %get-tuple-element.7.refs_1_, bf16[256,512]{1,0:T(8,128)(2,1)} %get-tuple-element.8.refs_2_), custom_call_target="tpu_custom_call" | custom-call | tf_op jit(solution)/shard_map/pallas_call | solution.py:906

commit v6 on v5

--- a/solution.py
+++ b/solution.py
@@ -243,7 +243,14 @@
 
     def start(self):
         self.box[self.me] = self.source[self.me]
-        each(1, self.count, lambda d: self.copy((self.me + d) % self.count, self.me).start())
+        half = self.count // 2
+
+        def one(d):
+            self.copy((self.me + half + d) % self.count, self.me).start()
+            self.copy((self.me + half - d) % self.count, self.me).start()
+
+        self.copy((self.me + half) % self.count, self.me).start()
+        each(1, half, one)
 
     def wait(self):
         def one(d):
@@ -388,6 +395,8 @@
     weight_sem,
     place_ref,
     placet_ref,
+    group_ref,
+    groupt_ref,
     drive,
     y,
     gated,
@@ -455,7 +464,7 @@
         flat = boxes[kind].reshape(exp_count * slab_rows, slab_width)
         return [
             jnp.dot(
-                regroup(q, 2 * rows, slots, False), flat, preferred_element_type=f32
+                group_ref[q], flat, preferred_element_type=f32
             ).astype(bf16)
             for q in range(4)
         ]
@@ -465,7 +474,7 @@
         for q in range(4):
             tile = slice(q * slab_width, (q + 1) * slab_width)
             term = jnp.dot(
-                regroup(q, 2 * rows, slots, True), read(tile), preferred_element_type=f32
+                groupt_ref[q], read(tile), preferred_element_type=f32
             )
             total = term if total is None else total + term
         to_slabs(kind, total)
@@ -590,6 +599,8 @@
         end16[:, tile] = h.astype(bf16)
     ends.start(ctx + 1, ctx_count)
     spread_lanes(c_ref, crep_ref)
+    for q in range(4):
+        group_ref[q] = regroup(q, 2 * rows, slots, False)
     moves[COT].wait()
     take_in(1, COT)
 
@@ -688,6 +699,8 @@
     spread = place_ref[0] + place_ref[1]
     to_slabs(ROW, jnp.dot(spread, quarters(normed), preferred_element_type=f32))
     moves[ROW].start()
+    for q in range(4):
+        groupt_ref[q] = regroup(q, 2 * rows, slots, True)
     for g in far_gathers[1]:
         g.before()
         g.after()
@@ -945,6 +958,8 @@
             dma((4,)),
             vm((2, 4 * exp_count * slots, 4 * my_rows), bf16),
             vm((2, 4 * my_rows, 4 * exp_count * slots), bf16),
+            vm((4, exp_count * slots, 4 * exp_count * slots), bf16),
+            vm((4, 4 * exp_count * slots, exp_count * slots), bf16),
             plane,
             plane,
             vm((seg_rows, channels), bf16),

time: 152 us -> 150 us (0.987)
  no operation moved by 1% of the time
where the time goes in v6:
time: 150 us
  Pallas kernels  149 us (99%)
    pallas_call x1, Pallas kernels, layer(): pl.pallas_call(layer_kernel, out_shape=[shape((my_rows, width), bf16), sh...  148 us

profile of v6, /device:TPU:1, one launch (start us, length us, event | category | flops | bytes accessed | tf_op | source)
XLA Modules:
  0.0 150.1 jit_solution(14672690220292139195)
XLA Ops:
  0.6 147.6 %shard_map.175 = (bf16[16,2048]{1,0:T(8,128)(2,1)}, bf16[16,2048]{1,0:T(8,128)(2,1)}, bf16[256,512]{1,0:T(8,128)(2,1)}) custom-call(f32[256,512]{1,0:T(8,128)} %delta_ref.1, bf16[256,512]{1,0:T(8,128)(2,1)} %u_ref.1, bf16[256,512]{1,0:T(8,128)(2,1)} %z_ref.1, f32[16,256]{1,0:T(8,128)} %bitcast.12, f32[16,256]{1,0:T(8,128)} %bitcast.13, ...), custom_call_target="tpu_custom_call" | custom-call | tf_op jit(solution)/shard_map/pallas_call | solution.py:941
  148.3 1.8 %shard_map.176 = (bf16[16,2048]{1,0:T(8,128)(2,1)}, bf16[16,2048]{1,0:T(8,128)(2,1)}, bf16[256,512]{1,0:T(8,128)(2,1)}) custom-call(bf16[16,2048]{1,0:T(8,128)(2,1)} %get-tuple-element.6.refs_0_, bf16[16,2048]{1,0:T(8,128)(2,1)} %get-tuple-element.7.refs_1_, bf16[256,512]{1,0:T(8,128)(2,1)} %get-tuple-element.8.refs_2_), custom_call_target="tpu_custom_call" | custom-call | tf_op jit(solution)/shard_map/pallas_call | solution.py:919
